TPU v7x, 128 devices: a whole 4x4x4 slice. The times are simulated.
128 devices in a mesh: led: 32 (over y, x, core), tile: 4 (over z).
Axes of the slice: x: 4, y: 4, z: 4, core: 2. Of those that a mesh axis runs over, the one named last changes fastest.
Arguments:
- spectrum: bfloat16 [1024, 2048], replicated, may hold values from -6 to 6
- pupils: bfloat16 [4, 512, 1024], replicated, may hold values from -1.5 to 1.5
- offsets: int32 [128, 2], P(('led', 'tile')), may hold values from 0 to 512
- measured: bfloat16 [128, 512, 512], P(('led', 'tile')), may hold values from 0.099609375 to 4
Outputs:
- spectrum_grad: float32 [4, 256, 2048], P('tile', 'led')
- pupil_grad: float32 [4, 512, 1024], P(None, 'led')
Inputs may be any that keep to these rules, and one draw needn't show every extreme that they name: `offsets`: each patch lies inside the spectrum.
All inputs are finite; a program needn't handle non-finite values.
Results may differ from a plain program's by a relative error of at most 0.011.
Values sent between devices are 32-bit elements; how exact they have to be, the bound alone decides.
A program may use at most 128 MiB of HBM per device.

v0:
```python
import math

import jax
import jax.numpy as jnp
import numpy as np
from jax import lax
from jax.experimental import pallas as pl
from jax.experimental.pallas import tpu as pltpu
from jax.sharding import PartitionSpec as P

MESH = pl.DeviceIdType.MESH
N = 512
H = 256
MODES = 4
SPEC = 1024
F32 = jnp.float32
BF16 = jnp.bfloat16

DIMS = (("y", 0), ("x", 0), ("z", 0), ("y", 1), ("x", 1), ("z", 1))

PUPIL_PHASES = (
    (0, 1, 2, 3),
    (4, 5, 0, 1),
    (2, 3, 4, 5),
    (0, 1, 2, 3),
)
CANVAS_PHASES = (
    (0, 1, 2, 3, 4, 4, 5, 5),
    (0, 1, 2, 2, 3, 3, 4, 5),
)
STREAMS = 6


def plan():
    counts = [0] * STREAMS
    place = {}
    groups = []
    for number, streams in enumerate(PUPIL_PHASES + CANVAS_PHASES):
        first = list(counts)
        for unit, stream in enumerate(streams):
            place[number, unit] = (stream, counts[stream])
            counts[stream] += 1
        for stream in range(STREAMS):
            if counts[stream] > first[stream]:
                groups.append((number, stream, first[stream], counts[stream]))
    return counts, place, groups


COUNTS, PLACE, GROUPS = plan()


def tables():
    positions = np.arange(N, dtype=np.int64)
    angles = (positions[:, None] * positions[None, :] % N).astype(np.float32) * np.float32(2.0 * math.pi / N)
    factor = np.float32(1.0 / math.sqrt(N))
    cosine = (np.cos(angles) * factor).astype(BF16)
    sine = (np.sin(angles) * factor).astype(BF16)
    half = np.concatenate([cosine[:H], sine[:H]], axis=0)
    half[H] = cosine[H]
    swap = np.zeros((H, H), np.float32)
    swap[(H - np.arange(H)) % H, np.arange(H)] = 1.0
    return half, np.ascontiguousarray(half.T), swap.astype(BF16)


def low_bit(position):
    return ((position + 1) // 2) % 2


def high_bit(position):
    return position // 2


def bits_of(y, x, z):
    return {
        ("y", 0): low_bit(y), ("y", 1): high_bit(y),
        ("x", 0): low_bit(x), ("x", 1): high_bit(x),
        ("z", 0): low_bit(z), ("z", 1): high_bit(z),
    }


def slot_of(bits, stream):
    slot = 0
    for step in range(6):
        slot = slot * 2 + bits[DIMS[(stream + step) % 6]]
    return slot


def dot(a, b):
    return jnp.dot(a, b, preferred_element_type=F32)


def kernel(mark, patch, pup, meas, tab, tabt, swap, out_spec, out_pup, *scratch):
    (half_s, field, inten, measp, xs, grads, folded, shift_rows, shift_cols, parts, parts_t, part, part_mark,
     peer, pupil_src, canvas_src) = scratch[:16]
    own = scratch[16:22]
    landed = scratch[22:28]
    (core_send, core_recv, send, recv, gather_send, gather_recv) = scratch[28:]

    led = lax.axis_index("led")
    z = lax.axis_index("tile")
    core = led % 2
    x = (led // 2) % 4
    y = led // 8
    other = 1 - core

    def device(yy, xx, cc, zz):
        return ((yy * 4 + xx) * 2 + cc, zz)

    def low(p):
        return p + 1 - 2 * (p % 2)

    def high(p):
        return 3 - p

    neighbour = {
        ("y", 0): device(low(y), x, core, z), ("y", 1): device(high(y), x, core, z),
        ("x", 0): device(y, low(x), core, z), ("x", 1): device(y, high(x), core, z),
        ("z", 0): device(y, x, core, low(z)), ("z", 1): device(y, x, core, high(z)),
    }
    partner = device(y, x, other, z)
    mine = bits_of(y, x, z)
    column = [(c, d) for d in range(4) for c in range(2) if (c, d) != (0, 0)]

    barrier = pltpu.get_barrier_semaphore()
    greeted = [neighbour["y", 0], neighbour["y", 1], neighbour["x", 0], neighbour["x", 1]]
    greeted += [device(y, x, (core + c) % 2, (z + d) % 4) for c, d in column]
    for target in greeted:
        pl.semaphore_signal(barrier, inc=1, device_id=target, device_id_type=MESH)

    measp[:, :H] = meas[0, :, :H]
    measp[:, H:] = dot(meas[0, :, H:], swap[...]).astype(BF16)
    measp[H:, :] = dot(swap[...], measp[H:, :]).astype(BF16)
    inten[...] = jnp.zeros_like(inten)

    lane0 = lax.broadcasted_iota(jnp.int32, (1, 128), 1) == 0
    row0 = lax.broadcasted_iota(jnp.int32, (16, 1), 0) == 0

    def forward(m, carry):
        for c in range(2):
            cols = slice(c * H, (c + 1) * H)
            cols_i = slice(N + c * H, N + (c + 1) * H)
            pr = patch[:, cols].astype(F32)
            pi = patch[:, cols_i].astype(F32)
            qr = pup[m, :, cols].astype(F32)
            qi = pup[m, :, cols_i].astype(F32)
            er = (pr * qr - pi * qi).astype(BF16)
            ei = (pr * qi + pi * qr).astype(BF16)
            u = dot(tab[...], er)
            v = dot(tab[...], ei)
            half_s[0, :H, cols] = (u[:H] - v[H:]).astype(BF16)
            half_s[0, H:, cols] = (u[:H] + v[H:]).astype(BF16)
            half_s[1, :H, cols] = (v[:H] + u[H:]).astype(BF16)
            half_s[1, H:, cols] = (v[:H] - u[H:]).astype(BF16)
            ut, ub, vt, vb = u[:16], u[H:H + 16], v[:16], v[H:H + 16]
            half_s[0, :16, cols] = jnp.where(row0, ut, ut - vb).astype(BF16)
            half_s[0, H:H + 16, cols] = jnp.where(row0, ub, ut + vb).astype(BF16)
            half_s[1, :16, cols] = jnp.where(row0, vt, vt + ub).astype(BF16)
            half_s[1, H:H + 16, cols] = jnp.where(row0, vb, vt - ub).astype(BF16)
        for r in range(2):
            rows = slice(r * H, (r + 1) * H)
            u = dot(half_s[0, rows, :], tabt[...])
            v = dot(half_s[1, rows, :], tabt[...])
            for b in range(2):
                left = slice(b * 128, (b + 1) * 128)
                right = slice(H + b * 128, H + (b + 1) * 128)
                uc, us, vc, vs = u[:, left], u[:, right], v[:, left], v[:, right]
                rl, il, rr, ir = uc - vs, vc + us, uc + vs, vc - us
                if b == 0:
                    rl = jnp.where(lane0, uc, rl)
                    il = jnp.where(lane0, vc, il)
                    rr = jnp.where(lane0, us, rr)
                    ir = jnp.where(lane0, vs, ir)
                field[0, m, rows, left] = rl
                field[1, m, rows, left] = il
                field[0, m, rows, right] = rr
                field[1, m, rows, right] = ir
                inten[rows, left] += rl * rl + il * il
                inten[rows, right] += rr * rr + ir * ir
        return carry

    lax.fori_loop(0, MODES, forward, 0)

    def weigh(i, carry):
        rows = pl.ds(pl.multiple_of(i * 64, 64), 64)
        level = measp[rows, :].astype(F32)
        inten[rows, :] = 1.0 - level * lax.rsqrt(level * jnp.maximum(inten[rows, :], 0.1))
        return carry

    lax.fori_loop(0, N // 64, weigh, 0)

    def backward(m):
        def fold(i, carry):
            top = pl.ds(pl.multiple_of(i * 32, 32), 32)
            bottom = pl.ds(pl.multiple_of(H + i * 32, 32), 32)
            wt, wb = inten[top, :], inten[bottom, :]
            rt, rb = wt * field[0, m, top, :], wb * field[0, m, bottom, :]
            it, ib = wt * field[1, m, top, :], wb * field[1, m, bottom, :]
            xs[0, top, :] = (rt + rb).astype(BF16)
            xs[0, bottom, :] = (it - ib).astype(BF16)
            xs[1, top, :] = (it + ib).astype(BF16)
            xs[1, bottom, :] = (rb - rt).astype(BF16)
            return carry

        lax.fori_loop(0, H // 32, fold, 0)
        wt, wb = inten[:16, :], inten[H:H + 16, :]
        rt, rb = wt * field[0, m, :16, :], wb * field[0, m, H:H + 16, :]
        it, ib = wt * field[1, m, :16, :], wb * field[1, m, H:H + 16, :]
        xs[0, :16, :] = jnp.where(row0, rt, rt + rb).astype(BF16)
        xs[0, H:H + 16, :] = jnp.where(row0, rb, it - ib).astype(BF16)
        xs[1, :16, :] = jnp.where(row0, it, it + ib).astype(BF16)
        xs[1, H:H + 16, :] = jnp.where(row0, ib, rb - rt).astype(BF16)

        def rows_of(i, carry):
            rows = pl.ds(pl.multiple_of(i * H, H), H)
            fr = dot(tabt[rows, :], xs[0])
            fi = dot(tabt[rows, :], xs[1])
            for b in range(2):
                left = slice(b * 128, (b + 1) * 128)
                right = slice(H + b * 128, H + (b + 1) * 128)
                rl, rr, il, ir = fr[:, left], fr[:, right], fi[:, left], fi[:, right]
                pr, mi, p_i, mr = rl + rr, il - ir, il + ir, rr - rl
                if b == 0:
                    pr = jnp.where(lane0, rl, pr)
                    mi = jnp.where(lane0, rr, mi)
                    p_i = jnp.where(lane0, il, p_i)
                    mr = jnp.where(lane0, ir, mr)
                half_s[0, rows, left] = pr.astype(BF16)
                half_s[0, rows, right] = mi.astype(BF16)
                half_s[1, rows, left] = p_i.astype(BF16)
                half_s[1, rows, right] = mr.astype(BF16)
            gr = dot(half_s[0, rows, :], tab[...])
            gi = dot(half_s[1, rows, :], tab[...])
            qr, qi = pup[m, rows, :N].astype(F32), pup[m, rows, N:].astype(F32)
            sr = qr * gr + qi * gi
            si = qr * gi - qi * gr
            if m == 0:
                grads[0, rows, :] = sr
                grads[1, rows, :] = si
            else:
                grads[0, rows, :] += sr
                grads[1, rows, :] += si
            pr, pi = patch[rows, :N].astype(F32), patch[rows, N:].astype(F32)
            field[0, m, rows, :] = pr * gr + pi * gi
            field[1, m, rows, :] = pr * gi - pi * gr
            return carry

        lax.fori_loop(0, 2, rows_of, 0)

    def core_copy(m):
        return pltpu.make_async_remote_copy(
            src_ref=field.at[other, m], dst_ref=peer.at[m], send_sem=core_send.at[m],
            recv_sem=core_recv.at[m], device_id=partner, device_id_type=MESH)

    def starts(stream):
        begin, out = 0, []
        for step in range(6):
            bit = mine[DIMS[(stream + step) % 6]]
            length = 32 >> step
            out.append((begin + bit * length, begin + (1 - bit) * length, length, 64 - 2 * length))
            begin = begin + bit * length
        return out, begin

    ranges = [starts(stream) for stream in range(STREAMS)]

    def hop(index, step):
        _, stream, first, last = GROUPS[index]
        _, away, length, offset = ranges[stream][0][step]
        units = pl.ds(first, last - first)
        return pltpu.make_async_remote_copy(
            src_ref=own[stream].at[units, pl.ds(away, length)],
            dst_ref=landed[stream].at[units, pl.ds(offset, length)],
            send_sem=send.at[index, step], recv_sem=recv.at[index, step],
            device_id=neighbour[DIMS[(stream + step) % 6]], device_id_type=MESH)

    def launch(phase):
        for index, group in enumerate(GROUPS):
            if group[0] == phase:
                hop(index, 0).start()

    def advance(phase, step):
        for index, (number, stream, first, last) in enumerate(GROUPS):
            if number != phase:
                continue
            hop(index, step).wait()
            keep, _, length, offset = ranges[stream][0][step]
            for unit in range(first, last):
                own[stream][unit, pl.ds(keep, length)] += landed[stream][unit, pl.ds(offset, length)]
            if step < 5:
                hop(index, step + 1).start()

    def spread_pupil(m):
        core_copy(m).wait()

        def body(yx, carry):
            for zz in range(4):
                bits = bits_of(yx // 4, yx % 4, zz)
                cols = slice(zz * 128, (zz + 1) * 128)
                for g in range(4):
                    stream, unit = PLACE[m, g]
                    rows = pl.ds(pl.multiple_of(yx * 32 + g * 8, 8), 8)
                    own[stream][unit, slot_of(bits, stream)] = field[core, m, rows, cols] + peer[m, rows, cols]
            return carry

        lax.fori_loop(0, 16, body, 0)
        launch(m)

    backward(0)
    pl.semaphore_wait(barrier, len(greeted))
    core_copy(0).start()
    backward(1)
    core_copy(1).start()
    spread_pupil(0)
    backward(2)
    core_copy(2).start()
    spread_pupil(1)
    advance(0, 0)
    backward(3)
    core_copy(3).start()
    advance(0, 1)
    advance(1, 0)
    spread_pupil(2)

    along = lax.broadcasted_iota(jnp.int32, (N, 128), 1).astype(F32)
    down = lax.broadcasted_iota(jnp.int32, (N, 128), 0).astype(F32)

    def wrap(value):
        return jnp.where(value >= float(N), value - float(N), value)

    for b in range(8):
        at = slice(b * 128, (b + 1) * 128)
        to = wrap(wrap(along + float(b % 4 * 128)) + mark[0, :1, :])
        shift_rows[:, at] = (down == wrap(to)).astype(F32).astype(BF16)
    for b in range(4):
        at = slice(b * 128, (b + 1) * 128)
        to = wrap(wrap(down + mark[1, :1, :]))
        hit = (along + float(b * 128) == to).astype(F32).astype(BF16)
        shift_cols[:N, at] = hit
        shift_cols[N:, at] = hit
    for part_no in range(2):
        whole = grads[part_no]
        coarse = whole.astype(BF16)
        parts[:N, :] = coarse
        parts[N:, :] = (whole - coarse.astype(F32)).astype(BF16)
        whole = dot(shift_rows[...], parts[...])
        coarse = whole.astype(BF16)
        parts_t[:, :N] = coarse
        parts_t[:, N:] = (whole - coarse.astype(F32)).astype(BF16)
        folded[part_no] = dot(parts_t[...], shift_cols[...])

    part_copy = pltpu.make_async_remote_copy(
        src_ref=folded.at[other], dst_ref=part, send_sem=core_send.at[4],
        recv_sem=core_recv.at[4], device_id=partner, device_id_type=MESH)
    mark_copy = pltpu.make_async_remote_copy(
        src_ref=mark, dst_ref=part_mark, send_sem=core_send.at[5],
        recv_sem=core_recv.at[5], device_id=partner, device_id_type=MESH)
    part_copy.start()
    mark_copy.start()
    spread_pupil(3)
    advance(0, 2)
    advance(1, 1)
    advance(2, 0)
    part_copy.wait()
    mark_copy.wait()

    iota_r = lax.broadcasted_iota(jnp.int32, (8, 128), 0).astype(F32)
    iota_c = lax.broadcasted_iota(jnp.int32, (8, 128), 1).astype(F32)

    def window(yx, carry):
        bit_sets = [bits_of(yx // 4, yx % 4, zz) for zz in range(4)]
        for zz in range(2):
            for g in range(2):
                base = 256 * zz + yx * 16 + g * 8
                rows = pl.ds(pl.multiple_of(base, 8), 8)
                row_no = iota_r + base.astype(F32)
                row_a = row_no < mark[0]
                row_b = row_no < part_mark[0]
                for block in range(4):
                    cols = slice(block * 128, (block + 1) * 128)
                    col_no = iota_c + float(block * 128)
                    col_a = col_no < mark[1]
                    col_b = col_no < part_mark[1]
                    value_a = folded[core, rows, cols]
                    value_b = part[rows, cols]
                    ra1 = jnp.where(row_a, value_a, 0.0)
                    ra0 = value_a - ra1
                    rb1 = jnp.where(row_b, value_b, 0.0)
                    rb0 = value_b - rb1
                    for upper, (va, vb) in enumerate(((ra0, rb0), (ra1, rb1))):
                        va1 = jnp.where(col_a, va, 0.0)
                        vb1 = jnp.where(col_b, vb, 0.0)
                        tiles = ((va - va1) + (vb - vb1), va1 + vb1)
                        bits = bit_sets[2 * upper + zz]
                        for later in range(2):
                            stream, unit = PLACE[4 + later, g * 4 + block]
                            own[stream][unit, slot_of(bits, stream)] = tiles[later]
        return carry

    lax.fori_loop(0, 16, window, 0)
    launch(4)
    launch(5)

    for phase, step in ((0, 3), (1, 2), (2, 1), (3, 0), (0, 4), (1, 3), (2, 2), (3, 1), (0, 5), (1, 4), (2, 3), (3, 2),
                        (1, 5), (2, 4), (4, 0), (3, 3), (2, 5), (5, 0), (3, 4), (4, 1), (3, 5)):
        advance(phase, step)

    for m in range(MODES):
        for g in range(4):
            stream, unit = PLACE[m, g]
            pupil_src[m, g * 8:(g + 1) * 8, :] = own[stream][unit, ranges[stream][1]]
    block = pl.ds(pl.multiple_of((core * 4 + z) * 128, 128), 128)
    copies = []
    for number, (c, d) in enumerate(column):
        to_core = (core + c) % 2
        copies.append(pltpu.make_async_remote_copy(
            src_ref=pupil_src.at[:, pl.ds(pl.multiple_of(to_core * 16, 16), 16), :],
            dst_ref=out_pup.at[:, :, block],
            send_sem=gather_send.at[number], recv_sem=gather_recv.at[number],
            device_id=device(y, x, to_core, (z + d) % 4), device_id_type=MESH))
        copies[-1].start()
    out_pup[:, :, block] = pupil_src[:, pl.ds(pl.multiple_of(core * 16, 16), 16), :]

    for phase, step in ((5, 1), (4, 2), (5, 2), (4, 3), (5, 3), (4, 4), (5, 4), (4, 5), (5, 5)):
        advance(phase, step)

    for phase in range(2):
        for g in range(2):
            for b in range(4):
                stream, unit = PLACE[4 + phase, g * 4 + b]
                at = (phase * 4 + b) * 128
                canvas_src[g, :, at:at + 128] = own[stream][unit, ranges[stream][1]]
    half_cols = pl.ds(pl.multiple_of(core * SPEC, SPEC), SPEC)
    last = pltpu.make_async_remote_copy(
        src_ref=canvas_src.at[other], dst_ref=out_spec.at[0, :, half_cols],
        send_sem=gather_send.at[7], recv_sem=gather_recv.at[7], device_id=partner, device_id_type=MESH)
    last.start()
    out_spec[0, :, half_cols] = canvas_src[core]
    for copy in copies:
        copy.wait()
    last.wait()


def local(spectrum, pupils, offsets, measured):
    row, col = offsets[0, 0], offsets[0, 1]
    patch = jnp.concatenate(
        [lax.dynamic_slice(spectrum, (row, col), (N, N)), lax.dynamic_slice(spectrum, (row, col + SPEC), (N, N))],
        axis=1)
    mark = jnp.broadcast_to(offsets.reshape(2, 1, 1).astype(F32), (2, 8, 128))
    half, half_t, swap = (jnp.asarray(table) for table in tables())
    vmem = pl.BlockSpec(memory_space=pltpu.VMEM)
    scratch = [
        pltpu.VMEM((2, N, N), BF16),
        pltpu.VMEM((2, MODES, N, N), F32),
        pltpu.VMEM((N, N), F32),
        pltpu.VMEM((N, N), BF16),
        pltpu.VMEM((2, N, N), BF16),
        pltpu.VMEM((2, N, N), F32),
        pltpu.VMEM((2, N, N), F32),
        pltpu.VMEM((N, 2 * N), BF16),
        pltpu.VMEM((2 * N, N), BF16),
        pltpu.VMEM((2 * N, N), BF16),
        pltpu.VMEM((N, 2 * N), BF16),
        pltpu.VMEM((N, N), F32),
        pltpu.VMEM((2, 8, 128), F32),
        pltpu.VMEM((MODES, N, N), F32),
        pltpu.VMEM((MODES, 32, 128), F32),
        pltpu.VMEM((2, 8, SPEC), F32),
    ]
    scratch += [pltpu.VMEM((count, 64, 8, 128), F32) for count in COUNTS]
    scratch += [pltpu.VMEM((count, 63, 8, 128), F32) for count in COUNTS]
    scratch += [pltpu.SemaphoreType.DMA((6,)), pltpu.SemaphoreType.DMA((6,))]
    scratch += [pltpu.SemaphoreType.DMA((len(GROUPS), 6)), pltpu.SemaphoreType.DMA((len(GROUPS), 6))]
    scratch += [pltpu.SemaphoreType.DMA((8,)), pltpu.SemaphoreType.DMA((8,))]
    return tuple(pl.pallas_call(
        kernel,
        out_shape=(
            jax.ShapeDtypeStruct((1, 8, 2 * SPEC), F32),
            jax.ShapeDtypeStruct((MODES, 16, 2 * N), F32),
        ),
        in_specs=[vmem] * 7,
        out_specs=(vmem, vmem),
        scratch_shapes=scratch,
        compiler_params=pltpu.CompilerParams(
            collective_id=0, has_side_effects=True, vmem_limit_bytes=60 * 2**20),
    )(mark, patch, pupils, measured, half, half_t, swap))


def solution(mesh):
    return jax.shard_map(
        local,
        mesh=mesh,
        in_specs=(P(), P(), P(("led", "tile"), None), P(("led", "tile"), None, None)),
        out_specs=(P("tile", "led", None), P(None, "led", None)),
        check_vma=False,
    )
```

profile of v0, /device:TPU:1, one launch (start us, length us, event | category | flops | bytes accessed | tf_op | source)
XLA Modules:
  0.0 100.0 jit_solution(4956176674339267097)
XLA Ops:
  0.6 0.0 copy-start
  0.6 1.3 %fusion.1 = (s32[1,1]{1,0:T(1,128)}, s32[1,1]{1,0:T(1,128)}) fusion(s32[1,2]{1,0:T(1,128)} %param.9), kind=kLoop, calls=%fused_computation.3 | loop fusion | bytes 16 | tf_op jit(solution)/shard_map/slice | solution.py:443
  7.2 1.9 %fusion = (bf16[512,512]{1,0:T(8,128)(2,1)S(1)}, bf16[512,512]{1,0:T(8,128)(2,1)S(1)}) fusion(bf16[1024,2048]{1,0:T(8,128)(2,1)} %param.7, s32[]{:T(128)S(6)} %select_n.10, s32[]{:T(128)S(6)} %select_n.11, s32[]{:T(128)S(6)} %select_n.12), kind=kLoop, calls=%fused_computation.2 | loop fusion | bytes 2097164 | tf_op jit(solution)/shard_map/dynamic_slice | solution.py:445
  9.1 1.1 %pad_maximum_fusion.patch = bf16[512,1024]{1,0:T(8,128)(2,1)} fusion(bf16[512,512]{1,0:T(8,128)(2,1)S(1)} %get-tuple-element.3, bf16[512,512]{1,0:T(8,128)(2,1)S(1)} %get-tuple-element.2), kind=kLoop, calls=%fused_computation | loop fusion | flops 2097152 | bytes 2097152 | tf_op jit(solution)/shard_map/concatenate | solution.py:444
  10.2 0.0 copy-done
  10.2 0.7 broadcast_in_dim.2.mark
  10.8 86.0 %shard_map.86 = (f32[1,8,2048]{2,1,0:T(8,128)}, f32[4,16,1024]{2,1,0:T(8,128)}) custom-call(f32[2,8,128]{2,1,0:T(8,128)} %broadcast_in_dim.2.mark, bf16[512,1024]{1,0:T(8,128)(2,1)} %pad_maximum_fusion.patch, bf16[4,512,1024]{2,1,0:T(8,128)(2,1)} %pup.1, bf16[1,512,512]{2,1,0:T(8,128)(2,1)} %meas.1, bf16[512,512]{1,0:T(8,128)(2,1)} %constant.14.clone.tab, ...), custom_call_target="tpu_custom_call" | custom-call | tf_op jit(solution)/shard_map/pallas_call | solution.py:473
  96.9 1.5 %copy.11 = f32[1,8,2048]{2,1,0:T(8,128)} copy(f32[1,8,2048]{2,1,0:T(8,128)} %get-tuple-element.8) | data formatting | bytes 131072
  98.3 1.7 %copy.12 = f32[4,16,1024]{2,1,0:T(8,128)} copy(f32[4,16,1024]{2,1,0:T(8,128)} %get-tuple-element.9) | data formatting | bytes 524288
  (1 shorter events, 0.0 us)
Async XLA Ops:
  0.6 9.5 %copy-start = (s32[1,2]{1,0:T(1,128)S(1)}, s32[1,2]{1,0:T(1,128)}, u32[]{:S(2)}) copy-start(s32[1,2]{1,0:T(1,128)} %param.9) | copy-start | bytes 28
where the time goes:
time: 100 us
  Pallas kernels  86 us (86%)
  local copies, waits for them, and re-layouts  7.06 us (7%)
  between operations  5.83 us (6%)
  other arithmetic  1.1 us (1%)
    pallas_call x1, Pallas kernels, local(): pl.pallas_call(kernel, out_shape=(jax.ShapeDtypeStruct((1, 8, 2 * SPEC),...  86 us
    unnamed x4, local copies, waits for them, and re-layouts  3.15 us

commit v1 on v0

--- a/solution.py
+++ b/solution.py
@@ -18,35 +18,38 @@
 
 DIMS = (("y", 0), ("x", 0), ("z", 0), ("y", 1), ("x", 1), ("z", 1))
 
-PUPIL_PHASES = (
+STREAMS = 6
+PIECES = (
     (0, 1, 2, 3),
     (4, 5, 0, 1),
     (2, 3, 4, 5),
     (0, 1, 2, 3),
+    (0, 1, 2, 3, 4, 4, 5, 5, 0, 1, 2, 2, 3, 3, 4, 5),
 )
-CANVAS_PHASES = (
-    (0, 1, 2, 3, 4, 4, 5, 5),
-    (0, 1, 2, 2, 3, 3, 4, 5),
-)
-STREAMS = 6
+CANVAS = 4
+PHASES = ((0, 1, 2, 3), (4,))
 
 
 def plan():
     counts = [0] * STREAMS
-    place = {}
-    groups = []
-    for number, streams in enumerate(PUPIL_PHASES + CANVAS_PHASES):
+    place, pieces, phases = {}, {}, {}
+    for number, streams in enumerate(PIECES):
         first = list(counts)
         for unit, stream in enumerate(streams):
             place[number, unit] = (stream, counts[stream])
             counts[stream] += 1
         for stream in range(STREAMS):
             if counts[stream] > first[stream]:
-                groups.append((number, stream, first[stream], counts[stream]))
-    return counts, place, groups
-
-
-COUNTS, PLACE, GROUPS = plan()
+                pieces[number, stream] = (first[stream], counts[stream])
+    for number, members in enumerate(PHASES):
+        for stream in range(STREAMS):
+            spans = [pieces[member, stream] for member in members if (member, stream) in pieces]
+            if spans:
+                phases[number, stream] = (spans[0][0], spans[-1][1])
+    return counts, place, pieces, phases
+
+
+COUNTS, PLACE, PIECE_SPANS, PHASE_SPANS = plan()
 
 
 def tables():
@@ -89,12 +92,48 @@
     return jnp.dot(a, b, preferred_element_type=F32)
 
 
+def extract(offs, spectrum, patch, mark, window, aligned, sem):
+    row, col = offs[0, 0], offs[0, 1]
+    row_from = pl.multiple_of(jnp.minimum(row // 16 * 16, N - 16), 16)
+    col_from = pl.multiple_of(jnp.minimum(col // 128 * 128, N - 128), 128)
+    copies = [
+        pltpu.make_async_copy(
+            spectrum.at[pl.ds(row_from, N + 16), pl.ds(part * SPEC + col_from, N + 128)],
+            window.at[part], sem.at[part])
+        for part in range(2)
+    ]
+    for copy in copies:
+        copy.start()
+    mark[0] = jnp.full((8, 128), row, jnp.int32).astype(F32)
+    mark[1] = jnp.full((8, 128), col, jnp.int32).astype(F32)
+    down = row - row_from
+    up = (24 - down % 8) % 24
+    turn = (N + 128 - (col - col_from)) % (N + 128)
+    for part in range(2):
+        copies[part].wait()
+
+        def turn_rows(i, carry):
+            rows = pl.ds(pl.multiple_of(i * 16, 16), 16)
+            aligned[part, rows, :] = pltpu.roll(window[part, rows, :].astype(F32), turn, 1)[:, :N]
+            return carry
+
+        lax.fori_loop(0, N // 16 + 1, turn_rows, 0, unroll=3)
+
+        def move_rows(i, carry):
+            rows = pl.ds(pl.multiple_of(i * 16, 16), 16)
+            source = pl.ds(pl.multiple_of((i * 2 + down // 8) * 8, 8), 24)
+            patch[rows, part * N:(part + 1) * N] = pltpu.roll(aligned[part, source, :], up, 0)[:16].astype(BF16)
+            return carry
+
+        lax.fori_loop(0, N // 16, move_rows, 0, unroll=4)
+
+
 def kernel(mark, patch, pup, meas, tab, tabt, swap, out_spec, out_pup, *scratch):
     (half_s, field, inten, measp, xs, grads, folded, shift_rows, shift_cols, parts, parts_t, part, part_mark,
      peer, pupil_src, canvas_src) = scratch[:16]
     own = scratch[16:22]
     landed = scratch[22:28]
-    (core_send, core_recv, send, recv, gather_send, gather_recv) = scratch[28:]
+    (core_send, core_recv, send0, recv0, send, recv, gather_send, gather_recv) = scratch[28:]
 
     led = lax.axis_index("led")
     z = lax.axis_index("tile")
@@ -262,31 +301,46 @@
 
     ranges = [starts(stream) for stream in range(STREAMS)]
 
-    def hop(index, step):
-        _, stream, first, last = GROUPS[index]
+    def copy_tiles(stream, span, step, send_one, recv_one):
+        units = pl.ds(span[0], span[1] - span[0])
         _, away, length, offset = ranges[stream][0][step]
-        units = pl.ds(first, last - first)
         return pltpu.make_async_remote_copy(
             src_ref=own[stream].at[units, pl.ds(away, length)],
             dst_ref=landed[stream].at[units, pl.ds(offset, length)],
-            send_sem=send.at[index, step], recv_sem=recv.at[index, step],
+            send_sem=send_one, recv_sem=recv_one,
             device_id=neighbour[DIMS[(stream + step) % 6]], device_id_type=MESH)
 
-    def launch(phase):
-        for index, group in enumerate(GROUPS):
-            if group[0] == phase:
-                hop(index, 0).start()
+    def first_hop(piece, stream):
+        return copy_tiles(stream, PIECE_SPANS[piece, stream], 0, send0.at[piece, stream], recv0.at[piece, stream])
+
+    def hop(phase, stream, step):
+        return copy_tiles(stream, PHASE_SPANS[phase, stream], step,
+                          send.at[phase, stream, step], recv.at[phase, stream, step])
+
+    def launch(piece):
+        for stream in range(STREAMS):
+            if (piece, stream) in PIECE_SPANS:
+                first_hop(piece, stream).start()
+
+    def add_landed(stream, span, step):
+        keep, _, length, offset = ranges[stream][0][step]
+        for unit in range(*span):
+            own[stream][unit, pl.ds(keep, length)] += landed[stream][unit, pl.ds(offset, length)]
 
     def advance(phase, step):
-        for index, (number, stream, first, last) in enumerate(GROUPS):
-            if number != phase:
+        for stream in range(STREAMS):
+            if (phase, stream) not in PHASE_SPANS:
                 continue
-            hop(index, step).wait()
-            keep, _, length, offset = ranges[stream][0][step]
-            for unit in range(first, last):
-                own[stream][unit, pl.ds(keep, length)] += landed[stream][unit, pl.ds(offset, length)]
+            if step == 0:
+                for piece in PHASES[phase]:
+                    if (piece, stream) in PIECE_SPANS:
+                        first_hop(piece, stream).wait()
+                        add_landed(stream, PIECE_SPANS[piece, stream], 0)
+            else:
+                hop(phase, stream, step).wait()
+                add_landed(stream, PHASE_SPANS[phase, stream], step)
             if step < 5:
-                hop(index, step + 1).start()
+                hop(phase, stream, step + 1).start()
 
     def spread_pupil(m):
         core_copy(m).wait()
@@ -313,11 +367,8 @@
     backward(2)
     core_copy(2).start()
     spread_pupil(1)
-    advance(0, 0)
     backward(3)
     core_copy(3).start()
-    advance(0, 1)
-    advance(1, 0)
     spread_pupil(2)
 
     along = lax.broadcasted_iota(jnp.int32, (N, 128), 1).astype(F32)
@@ -336,7 +387,7 @@
         hit = (along + float(b * 128) == to).astype(F32).astype(BF16)
         shift_cols[:N, at] = hit
         shift_cols[N:, at] = hit
-    for part_no in range(2):
+    def roll(part_no):
         whole = grads[part_no]
         coarse = whole.astype(BF16)
         parts[:N, :] = coarse
@@ -353,12 +404,11 @@
     mark_copy = pltpu.make_async_remote_copy(
         src_ref=mark, dst_ref=part_mark, send_sem=core_send.at[5],
         recv_sem=core_recv.at[5], device_id=partner, device_id_type=MESH)
+    mark_copy.start()
+    roll(other)
     part_copy.start()
-    mark_copy.start()
     spread_pupil(3)
-    advance(0, 2)
-    advance(1, 1)
-    advance(2, 0)
+    roll(core)
     part_copy.wait()
     mark_copy.wait()
 
@@ -391,16 +441,14 @@
                         tiles = ((va - va1) + (vb - vb1), va1 + vb1)
                         bits = bit_sets[2 * upper + zz]
                         for later in range(2):
-                            stream, unit = PLACE[4 + later, g * 4 + block]
+                            stream, unit = PLACE[CANVAS, g * 8 + later * 4 + block]
                             own[stream][unit, slot_of(bits, stream)] = tiles[later]
         return carry
 
     lax.fori_loop(0, 16, window, 0)
-    launch(4)
-    launch(5)
-
-    for phase, step in ((0, 3), (1, 2), (2, 1), (3, 0), (0, 4), (1, 3), (2, 2), (3, 1), (0, 5), (1, 4), (2, 3), (3, 2),
-                        (1, 5), (2, 4), (4, 0), (3, 3), (2, 5), (5, 0), (3, 4), (4, 1), (3, 5)):
+    launch(CANVAS)
+
+    for phase, step in ((0, 0), (0, 1), (1, 0), (0, 2), (1, 1), (0, 3), (1, 2), (0, 4), (1, 3), (0, 5)):
         advance(phase, step)
 
     for m in range(MODES):
@@ -419,15 +467,13 @@
         copies[-1].start()
     out_pup[:, :, block] = pupil_src[:, pl.ds(pl.multiple_of(core * 16, 16), 16), :]
 
-    for phase, step in ((5, 1), (4, 2), (5, 2), (4, 3), (5, 3), (4, 4), (5, 4), (4, 5), (5, 5)):
-        advance(phase, step)
-
-    for phase in range(2):
-        for g in range(2):
-            for b in range(4):
-                stream, unit = PLACE[4 + phase, g * 4 + b]
-                at = (phase * 4 + b) * 128
-                canvas_src[g, :, at:at + 128] = own[stream][unit, ranges[stream][1]]
+    for step in (4, 5):
+        advance(1, step)
+
+    for g in range(2):
+        for b in range(8):
+            stream, unit = PLACE[CANVAS, g * 8 + b]
+            canvas_src[g, :, b * 128:(b + 1) * 128] = own[stream][unit, ranges[stream][1]]
     half_cols = pl.ds(pl.multiple_of(core * SPEC, SPEC), SPEC)
     last = pltpu.make_async_remote_copy(
         src_ref=canvas_src.at[other], dst_ref=out_spec.at[0, :, half_cols],
@@ -440,13 +486,20 @@
 
 
 def local(spectrum, pupils, offsets, measured):
-    row, col = offsets[0, 0], offsets[0, 1]
-    patch = jnp.concatenate(
-        [lax.dynamic_slice(spectrum, (row, col), (N, N)), lax.dynamic_slice(spectrum, (row, col + SPEC), (N, N))],
-        axis=1)
-    mark = jnp.broadcast_to(offsets.reshape(2, 1, 1).astype(F32), (2, 8, 128))
+    vmem = pl.BlockSpec(memory_space=pltpu.VMEM)
+    patch, mark = pl.pallas_call(
+        extract,
+        out_shape=(jax.ShapeDtypeStruct((N, 2 * N), BF16), jax.ShapeDtypeStruct((2, 8, 128), F32)),
+        in_specs=[pl.BlockSpec(memory_space=pltpu.SMEM), pl.BlockSpec(memory_space=pl.ANY)],
+        out_specs=(vmem, vmem),
+        scratch_shapes=[
+            pltpu.VMEM((2, N + 16, N + 128), BF16),
+            pltpu.VMEM((2, N + 24, N), F32),
+            pltpu.SemaphoreType.DMA((2,)),
+        ],
+        compiler_params=pltpu.CompilerParams(vmem_limit_bytes=16 * 2**20),
+    )(offsets, spectrum)
     half, half_t, swap = (jnp.asarray(table) for table in tables())
-    vmem = pl.BlockSpec(memory_space=pltpu.VMEM)
     scratch = [
         pltpu.VMEM((2, N, N), BF16),
         pltpu.VMEM((2, MODES, N, N), F32),
@@ -468,7 +521,8 @@
     scratch += [pltpu.VMEM((count, 64, 8, 128), F32) for count in COUNTS]
     scratch += [pltpu.VMEM((count, 63, 8, 128), F32) for count in COUNTS]
     scratch += [pltpu.SemaphoreType.DMA((6,)), pltpu.SemaphoreType.DMA((6,))]
-    scratch += [pltpu.SemaphoreType.DMA((len(GROUPS), 6)), pltpu.SemaphoreType.DMA((len(GROUPS), 6))]
+    scratch += [pltpu.SemaphoreType.DMA((len(PIECES), STREAMS)), pltpu.SemaphoreType.DMA((len(PIECES), STREAMS))]
+    scratch += [pltpu.SemaphoreType.DMA((len(PHASES), STREAMS, 6)), pltpu.SemaphoreType.DMA((len(PHASES), STREAMS, 6))]
     scratch += [pltpu.SemaphoreType.DMA((8,)), pltpu.SemaphoreType.DMA((8,))]
     return tuple(pl.pallas_call(
         kernel,

time: 100 us -> 86.8 us (0.87)
  Pallas kernels: 86 us -> 78.3 us
  between operations: 5.83 us -> 0.66 us
  other arithmetic: 1.1 us -> 0 us
    pallas_call x1, Pallas kernels: 86 us -> 74.9 us  [local(): pl.pallas_call(kernel, out_shape=(jax.ShapeDtypeStruct((1, 8, 2 * SPEC),...]
    unnamed x4 -> x10, local copies, waits for them, and re-layouts: 3.15 us -> 7.54 us
    pallas_call x0 -> x1, Pallas kernels: none -> 3.45 us  [local(): pl.pallas_call(extract, out_shape=(jax.ShapeDtypeStruct((N, 2 * N), BF16)...]
    dynamic_slice x1 -> x0, local copies, waits for them, and re-layouts: 1.9 us -> none  [local(): lax.dynamic_slice(spectrum, (row, col), (N, N))]
    slice x1 -> x0, local copies, waits for them, and re-layouts: 1.34 us -> none  [local(): row, col = (offsets[0, 0], offsets[0, 1])]
    concatenate x1 -> x0, other arithmetic: 1.1 us -> none  [local(): jnp.concatenate([lax.dynamic_slice(spectrum, (row, col), (N, N)), lax.dyn...]
where the time goes in v1:
time: 86.8 us; the launch traced here: 86.5 us
  Pallas kernels  78.3 us (90%)
  local copies, waits for them, and re-layouts  7.54 us (9%)
    pallas_call x1, Pallas kernels, local(): pl.pallas_call(kernel, out_shape=(jax.ShapeDtypeStruct((1, 8, 2 * SPEC),...  74.9 us
    unnamed x10, local copies, waits for them, and re-layouts  7.54 us
    pallas_call x1, Pallas kernels, local(): pl.pallas_call(extract, out_shape=(jax.ShapeDtypeStruct((N, 2 * N), BF16)...  3.45 us

profile of v1, /device:TPU:1, one launch (start us, length us, event | category | flops | bytes accessed | tf_op | source)
XLA Modules:
  0.0 86.5 jit_solution(8025482964348016724)
XLA Ops:
  0.6 0.0 copy-start
  0.6 2.2 %copy-done = bf16[1024,2048]{1,0:T(8,128)(2,1)S(1)} copy-done((bf16[1024,2048]{1,0:T(8,128)(2,1)S(1)}, bf16[1024,2048]{1,0:T(8,128)(2,1)}, u32[]{:S(2)}) %copy-start) | copy-done | bytes 4194328
  2.8 0.0 copy-start.3
  2.8 0.7 copy-done.3
  3.5 3.5 %shard_map.86 = (bf16[512,1024]{1,0:T(8,128)(2,1)S(1)}, f32[2,8,128]{2,1,0:T(8,128)S(1)}) custom-call(s32[1,2]{1,0:T(1,128)S(1)} %copy-done.3, bf16[1024,2048]{1,0:T(8,128)(2,1)S(1)} %copy-done), custom_call_target="tpu_custom_call" | custom-call | tf_op jit(solution)/shard_map/pallas_call | solution.py:490
  6.9 0.0 copy-start.1
  6.9 1.0 %copy-done.1 = bf16[512,1024]{1,0:T(8,128)(2,1)} copy-done((bf16[512,1024]{1,0:T(8,128)(2,1)}, bf16[512,1024]{1,0:T(8,128)(2,1)S(1)}, u32[]{:S(2)}) %copy-start.1) | copy-done | bytes 1048600
  7.9 0.0 copy-start.2
  7.9 0.6 copy-done.2
  8.5 74.9 %shard_map.87 = (f32[1,8,2048]{2,1,0:T(8,128)}, f32[4,16,1024]{2,1,0:T(8,128)}) custom-call(f32[2,8,128]{2,1,0:T(8,128)} %copy-done.2, bf16[512,1024]{1,0:T(8,128)(2,1)} %copy-done.1, bf16[4,512,1024]{2,1,0:T(8,128)(2,1)} %pup.1, bf16[1,512,512]{2,1,0:T(8,128)(2,1)} %meas.1, bf16[512,512]{1,0:T(8,128)(2,1)} %constant.6.clone.tab, ...), custom_call_target="tpu_custom_call" | custom-call | tf_op jit(solution)/shard_map/pallas_call | solution.py:527
  83.4 1.5 %copy.11 = f32[1,8,2048]{2,1,0:T(8,128)} copy(f32[1,8,2048]{2,1,0:T(8,128)} %get-tuple-element.8) | data formatting | bytes 131072
  84.9 1.7 %copy.12 = f32[4,16,1024]{2,1,0:T(8,128)} copy(f32[4,16,1024]{2,1,0:T(8,128)} %get-tuple-element.9) | data formatting | bytes 524288
Async XLA Ops:
  0.6 2.2 %copy-start = (bf16[1024,2048]{1,0:T(8,128)(2,1)S(1)}, bf16[1024,2048]{1,0:T(8,128)(2,1)}, u32[]{:S(2)}) copy-start(bf16[1024,2048]{1,0:T(8,128)(2,1)} %spectrum.1) | copy-start | bytes 12582916
  2.8 0.7 copy-start.3
  6.9 1.0 %copy-start.1 = (bf16[512,1024]{1,0:T(8,128)(2,1)}, bf16[512,1024]{1,0:T(8,128)(2,1)S(1)}, u32[]{:S(2)}) copy-start(bf16[512,1024]{1,0:T(8,128)(2,1)S(1)} %get-tuple-element.5.patch) | copy-start | bytes 3145732
  7.9 0.6 copy-start.2

commit v2 on v1

--- a/solution.py
+++ b/solution.py
@@ -16,7 +16,9 @@
 F32 = jnp.float32
 BF16 = jnp.bfloat16
 
-DIMS = (("y", 0), ("x", 0), ("z", 0), ("y", 1), ("x", 1), ("z", 1))
+ORDERS = (("y", 0, "x", "z"), ("x", 0, "z", "y"), ("z", 0, "y", "x"),
+          ("y", 1, "z", "x"), ("x", 1, "y", "z"), ("z", 1, "x", "y"))
+LEVELS = 4
 
 STREAMS = 6
 PIECES = (
@@ -27,7 +29,9 @@
     (0, 1, 2, 3, 4, 4, 5, 5, 0, 1, 2, 2, 3, 3, 4, 5),
 )
 CANVAS = 4
-PHASES = ((0, 1, 2, 3), (4,))
+PHASES = ((0, 1), (2, 3), (4,))
+BEFORE = ((0, 1), (1, 0), (2, 0), (0, 2), (1, 1), (2, 1), (0, 3), (1, 2), (2, 2), (1, 3))
+AFTER = ((2, 3),)
 
 
 def plan():
@@ -73,19 +77,10 @@
     return position // 2
 
 
-def bits_of(y, x, z):
-    return {
-        ("y", 0): low_bit(y), ("y", 1): high_bit(y),
-        ("x", 0): low_bit(x), ("x", 1): high_bit(x),
-        ("z", 0): low_bit(z), ("z", 1): high_bit(z),
-    }
-
-
-def slot_of(bits, stream):
-    slot = 0
-    for step in range(6):
-        slot = slot * 2 + bits[DIMS[(stream + step) % 6]]
-    return slot
+def slot_of(at, stream):
+    axis, bit, second, third = ORDERS[stream]
+    bits = low_bit(at[axis]), high_bit(at[axis])
+    return ((bits[bit] * 2 + bits[1 - bit]) * 4 + at[second]) * 4 + at[third]
 
 
 def dot(a, b):
@@ -128,12 +123,19 @@
         lax.fori_loop(0, N // 16, move_rows, 0, unroll=4)
 
 
-def kernel(mark, patch, pup, meas, tab, tabt, swap, out_spec, out_pup, *scratch):
-    (half_s, field, inten, measp, xs, grads, folded, shift_rows, shift_cols, parts, parts_t, part, part_mark,
-     peer, pupil_src, canvas_src) = scratch[:16]
-    own = scratch[16:22]
-    landed = scratch[22:28]
-    (core_send, core_recv, send0, recv0, send, recv, gather_send, gather_recv) = scratch[28:]
+def kernel(mark, patch, pupils, meas, tab, tabt, swap, out_spec, out_pup, *scratch):
+    (half_s, field, inten, measp, xs, grads, folded, shift_rows, shift_cols, parts, parts_t, peer_grad, part_mark,
+     peer, pupil_src, canvas_src, pup) = scratch[:17]
+    own = scratch[17:23]
+    landed = scratch[23:29]
+    (core_send, core_recv, send0, recv0, send, recv, gather_send, gather_recv, load) = scratch[29:]
+
+    def pupil_load(m):
+        return pltpu.make_async_copy(pupils.at[m], pup.at[m], load.at[m])
+
+    for m in range(MODES):
+        pupil_load(m).start()
+
 
     led = lax.axis_index("led")
     z = lax.axis_index("tile")
@@ -151,17 +153,17 @@
     def high(p):
         return 3 - p
 
-    neighbour = {
-        ("y", 0): device(low(y), x, core, z), ("y", 1): device(high(y), x, core, z),
-        ("x", 0): device(y, low(x), core, z), ("x", 1): device(y, high(x), core, z),
-        ("z", 0): device(y, x, core, low(z)), ("z", 1): device(y, x, core, high(z)),
-    }
+    here = {"y": y, "x": x, "z": z}
+
+    def moved(axis, position):
+        there = dict(here, **{axis: position})
+        return device(there["y"], there["x"], core, there["z"])
+
     partner = device(y, x, other, z)
-    mine = bits_of(y, x, z)
     column = [(c, d) for d in range(4) for c in range(2) if (c, d) != (0, 0)]
 
     barrier = pltpu.get_barrier_semaphore()
-    greeted = [neighbour["y", 0], neighbour["y", 1], neighbour["x", 0], neighbour["x", 1]]
+    greeted = [moved(axis, (here[axis] + k) % 4) for axis in ("y", "x") for k in range(1, 4)]
     greeted += [device(y, x, (core + c) % 2, (z + d) % 4) for c, d in column]
     for target in greeted:
         pl.semaphore_signal(barrier, inc=1, device_id=target, device_id_type=MESH)
@@ -175,6 +177,7 @@
     row0 = lax.broadcasted_iota(jnp.int32, (16, 1), 0) == 0
 
     def forward(m, carry):
+        pupil_load(m).wait()
         for c in range(2):
             cols = slice(c * H, (c + 1) * H)
             cols_i = slice(N + c * H, N + (c + 1) * H)
@@ -227,7 +230,7 @@
 
     lax.fori_loop(0, N // 64, weigh, 0)
 
-    def backward(m):
+    def weigh_fold(m):
         def fold(i, carry):
             top = pl.ds(pl.multiple_of(i * 32, 32), 32)
             bottom = pl.ds(pl.multiple_of(H + i * 32, 32), 32)
@@ -249,73 +252,87 @@
         xs[1, :16, :] = jnp.where(row0, it, it + ib).astype(BF16)
         xs[1, H:H + 16, :] = jnp.where(row0, ib, rb - rt).astype(BF16)
 
-        def rows_of(i, carry):
-            rows = pl.ds(pl.multiple_of(i * H, H), H)
-            fr = dot(tabt[rows, :], xs[0])
-            fi = dot(tabt[rows, :], xs[1])
-            for b in range(2):
-                left = slice(b * 128, (b + 1) * 128)
-                right = slice(H + b * 128, H + (b + 1) * 128)
-                rl, rr, il, ir = fr[:, left], fr[:, right], fi[:, left], fi[:, right]
-                pr, mi, p_i, mr = rl + rr, il - ir, il + ir, rr - rl
-                if b == 0:
-                    pr = jnp.where(lane0, rl, pr)
-                    mi = jnp.where(lane0, rr, mi)
-                    p_i = jnp.where(lane0, il, p_i)
-                    mr = jnp.where(lane0, ir, mr)
-                half_s[0, rows, left] = pr.astype(BF16)
-                half_s[0, rows, right] = mi.astype(BF16)
-                half_s[1, rows, left] = p_i.astype(BF16)
-                half_s[1, rows, right] = mr.astype(BF16)
-            gr = dot(half_s[0, rows, :], tab[...])
-            gi = dot(half_s[1, rows, :], tab[...])
-            qr, qi = pup[m, rows, :N].astype(F32), pup[m, rows, N:].astype(F32)
-            sr = qr * gr + qi * gi
-            si = qr * gi - qi * gr
-            if m == 0:
-                grads[0, rows, :] = sr
-                grads[1, rows, :] = si
-            else:
-                grads[0, rows, :] += sr
-                grads[1, rows, :] += si
-            pr, pi = patch[rows, :N].astype(F32), patch[rows, N:].astype(F32)
-            field[0, m, rows, :] = pr * gr + pi * gi
-            field[1, m, rows, :] = pr * gi - pi * gr
-            return carry
-
-        lax.fori_loop(0, 2, rows_of, 0)
-
-    def core_copy(m):
+    def transform(m, i):
+        rows = slice(i * H, (i + 1) * H)
+        fr = dot(tabt[rows, :], xs[0])
+        fi = dot(tabt[rows, :], xs[1])
+        for b in range(2):
+            left = slice(b * 128, (b + 1) * 128)
+            right = slice(H + b * 128, H + (b + 1) * 128)
+            rl, rr, il, ir = fr[:, left], fr[:, right], fi[:, left], fi[:, right]
+            pr, mi, p_i, mr = rl + rr, il - ir, il + ir, rr - rl
+            if b == 0:
+                pr = jnp.where(lane0, rl, pr)
+                mi = jnp.where(lane0, rr, mi)
+                p_i = jnp.where(lane0, il, p_i)
+                mr = jnp.where(lane0, ir, mr)
+            half_s[0, rows, left] = pr.astype(BF16)
+            half_s[0, rows, right] = mi.astype(BF16)
+            half_s[1, rows, left] = p_i.astype(BF16)
+            half_s[1, rows, right] = mr.astype(BF16)
+        gr = dot(half_s[0, rows, :], tab[...])
+        gi = dot(half_s[1, rows, :], tab[...])
+        qr, qi = pup[m, rows, :N].astype(F32), pup[m, rows, N:].astype(F32)
+        sr = qr * gr + qi * gi
+        si = qr * gi - qi * gr
+        if m == 0:
+            grads[0, rows, :] = sr
+            grads[1, rows, :] = si
+        else:
+            grads[0, rows, :] += sr
+            grads[1, rows, :] += si
+        pr, pi = patch[rows, :N].astype(F32), patch[rows, N:].astype(F32)
+        field[0, m, rows, :] = pr * gr + pi * gi
+        field[1, m, rows, :] = pr * gi - pi * gr
+
+    def core_copy(m, i):
+        rows = pl.ds(i * H, H)
         return pltpu.make_async_remote_copy(
-            src_ref=field.at[other, m], dst_ref=peer.at[m], send_sem=core_send.at[m],
-            recv_sem=core_recv.at[m], device_id=partner, device_id_type=MESH)
-
-    def starts(stream):
-        begin, out = 0, []
-        for step in range(6):
-            bit = mine[DIMS[(stream + step) % 6]]
-            length = 32 >> step
-            out.append((begin + bit * length, begin + (1 - bit) * length, length, 64 - 2 * length))
-            begin = begin + bit * length
-        return out, begin
-
-    ranges = [starts(stream) for stream in range(STREAMS)]
-
-    def copy_tiles(stream, span, step, send_one, recv_one):
+            src_ref=field.at[other, m, rows], dst_ref=peer.at[m, rows], send_sem=core_send.at[2 * m + i],
+            recv_sem=core_recv.at[2 * m + i], device_id=partner, device_id_type=MESH)
+
+    def copy_tiles(stream, span, away, length, offset, sems, target):
         units = pl.ds(span[0], span[1] - span[0])
-        _, away, length, offset = ranges[stream][0][step]
         return pltpu.make_async_remote_copy(
             src_ref=own[stream].at[units, pl.ds(away, length)],
             dst_ref=landed[stream].at[units, pl.ds(offset, length)],
-            send_sem=send_one, recv_sem=recv_one,
-            device_id=neighbour[DIMS[(stream + step) % 6]], device_id_type=MESH)
+            send_sem=sems[0], recv_sem=sems[1], device_id=target, device_id_type=MESH)
+
+    def halves(stream):
+        axis, bit, second, third = ORDERS[stream]
+        bits = low_bit(here[axis]), high_bit(here[axis])
+        one = bits[bit] * 32
+        return axis, bit, bits, one, one + bits[1 - bit] * 16
 
     def first_hop(piece, stream):
-        return copy_tiles(stream, PIECE_SPANS[piece, stream], 0, send0.at[piece, stream], recv0.at[piece, stream])
-
-    def hop(phase, stream, step):
-        return copy_tiles(stream, PHASE_SPANS[phase, stream], step,
-                          send.at[phase, stream, step], recv.at[phase, stream, step])
+        axis, bit, bits, _, _ = halves(stream)
+        return copy_tiles(stream, PIECE_SPANS[piece, stream], (1 - bits[bit]) * 32, 32, 0,
+                          (send0.at[piece, stream], recv0.at[piece, stream]),
+                          moved(axis, (low, high)[bit](here[axis])))
+
+    def hops(phase, stream, step):
+        span = PHASE_SPANS[phase, stream]
+        axis, bit, bits, one, two = halves(stream)
+
+        def sems(number):
+            return send.at[phase, stream, number], recv.at[phase, stream, number]
+
+        if step == 1:
+            return [copy_tiles(stream, span, one + (1 - bits[1 - bit]) * 16, 16, 32, sems(0),
+                               moved(axis, (low, high)[1 - bit](here[axis])))]
+        ring = ORDERS[stream][step]
+        out = []
+        for k in (2, 1, 3):
+            to = (here[ring] + k) % 4
+            if step == 2:
+                away, length, offset = two + to * 4, 4, 48 + 4 * (k - 1)
+            else:
+                away, length, offset = two + here[ORDERS[stream][2]] * 4 + to, 1, 60 + (k - 1)
+            out.append(copy_tiles(stream, span, away, length, offset, sems(3 * step - 6 + k), moved(ring, to)))
+        return out
+
+    def final_slot(stream):
+        return slot_of(here, stream)
 
     def launch(piece):
         for stream in range(STREAMS):
@@ -323,9 +340,16 @@
                 first_hop(piece, stream).start()
 
     def add_landed(stream, span, step):
-        keep, _, length, offset = ranges[stream][0][step]
+        _, _, _, one, two = halves(stream)
+        second, third = (here[axis] for axis in ORDERS[stream][2:])
+        keep, length, offset, count = (
+            (one, 32, 0, 1), (two, 16, 32, 1), (two + second * 4, 4, 48, 3),
+            (two + second * 4 + third, 1, 60, 3))[step]
         for unit in range(*span):
-            own[stream][unit, pl.ds(keep, length)] += landed[stream][unit, pl.ds(offset, length)]
+            total = own[stream][unit, pl.ds(keep, length)]
+            for k in range(count):
+                total += landed[stream][unit, pl.ds(offset + k * length, length)]
+            own[stream][unit, pl.ds(keep, length)] = total
 
     def advance(phase, step):
         for stream in range(STREAMS):
@@ -337,39 +361,53 @@
                         first_hop(piece, stream).wait()
                         add_landed(stream, PIECE_SPANS[piece, stream], 0)
             else:
-                hop(phase, stream, step).wait()
+                for copy in hops(phase, stream, step):
+                    copy.wait()
                 add_landed(stream, PHASE_SPANS[phase, stream], step)
-            if step < 5:
-                hop(phase, stream, step + 1).start()
+            if step < LEVELS - 1:
+                for copy in hops(phase, stream, step + 1):
+                    copy.start()
 
     def spread_pupil(m):
-        core_copy(m).wait()
+        core_copy(m, 0).wait()
+        core_copy(m, 1).wait()
 
         def body(yx, carry):
             for zz in range(4):
-                bits = bits_of(yx // 4, yx % 4, zz)
+                at = {"y": yx // 4, "x": yx % 4, "z": zz}
                 cols = slice(zz * 128, (zz + 1) * 128)
                 for g in range(4):
                     stream, unit = PLACE[m, g]
                     rows = pl.ds(pl.multiple_of(yx * 32 + g * 8, 8), 8)
-                    own[stream][unit, slot_of(bits, stream)] = field[core, m, rows, cols] + peer[m, rows, cols]
+                    own[stream][unit, slot_of(at, stream)] = field[core, m, rows, cols] + peer[m, rows, cols]
             return carry
 
         lax.fori_loop(0, 16, body, 0)
         launch(m)
 
-    backward(0)
-    pl.semaphore_wait(barrier, len(greeted))
-    core_copy(0).start()
-    backward(1)
-    core_copy(1).start()
-    spread_pupil(0)
-    backward(2)
-    core_copy(2).start()
-    spread_pupil(1)
-    backward(3)
-    core_copy(3).start()
-    spread_pupil(2)
+    def grad_copy(i):
+        rows = pl.ds(i * H, H)
+        return pltpu.make_async_remote_copy(
+            src_ref=grads.at[other, rows], dst_ref=peer_grad.at[rows],
+            send_sem=(core_send.at[8], core_send.at[10])[i], recv_sem=(core_recv.at[8], core_recv.at[10])[i],
+            device_id=partner, device_id_type=MESH)
+
+    mark_copy = pltpu.make_async_remote_copy(
+        src_ref=mark, dst_ref=part_mark, send_sem=core_send.at[9],
+        recv_sem=core_recv.at[9], device_id=partner, device_id_type=MESH)
+
+    def backward(m, between=()):
+        weigh_fold(m)
+        for i in range(2):
+            transform(m, i)
+            if m == 0 and i == 0:
+                pl.semaphore_wait(barrier, len(greeted))
+            if m == MODES - 1:
+                grad_copy(i).start()
+            core_copy(m, i).start()
+            if i == 0:
+                for task, *values in between:
+                    task(*values)
 
     along = lax.broadcasted_iota(jnp.int32, (N, 128), 1).astype(F32)
     down = lax.broadcasted_iota(jnp.int32, (N, 128), 0).astype(F32)
@@ -377,18 +415,20 @@
     def wrap(value):
         return jnp.where(value >= float(N), value - float(N), value)
 
-    for b in range(8):
-        at = slice(b * 128, (b + 1) * 128)
-        to = wrap(wrap(along + float(b % 4 * 128)) + mark[0, :1, :])
-        shift_rows[:, at] = (down == wrap(to)).astype(F32).astype(BF16)
-    for b in range(4):
-        at = slice(b * 128, (b + 1) * 128)
-        to = wrap(wrap(down + mark[1, :1, :]))
-        hit = (along + float(b * 128) == to).astype(F32).astype(BF16)
-        shift_cols[:N, at] = hit
-        shift_cols[N:, at] = hit
-    def roll(part_no):
-        whole = grads[part_no]
+    def one_hots(shifts):
+        for b in range(4):
+            at = slice(b * 128, (b + 1) * 128)
+            to = wrap(along[:1] + float(b * 128) + shifts[0, :1, :])
+            hit = (down == wrap(to)).astype(F32).astype(BF16)
+            shift_rows[:, at] = hit
+            shift_rows[:, N + b * 128:N + (b + 1) * 128] = hit
+            to = wrap(down + shifts[1, :1, :])
+            hit = (along + float(b * 128) == wrap(to)).astype(F32).astype(BF16)
+            shift_cols[:N, at] = hit
+            shift_cols[N:, at] = hit
+
+    def roll(whole, shifts, number):
+        one_hots(shifts)
         coarse = whole.astype(BF16)
         parts[:N, :] = coarse
         parts[N:, :] = (whole - coarse.astype(F32)).astype(BF16)
@@ -396,27 +436,25 @@
         coarse = whole.astype(BF16)
         parts_t[:, :N] = coarse
         parts_t[:, N:] = (whole - coarse.astype(F32)).astype(BF16)
-        folded[part_no] = dot(parts_t[...], shift_cols[...])
-
-    part_copy = pltpu.make_async_remote_copy(
-        src_ref=folded.at[other], dst_ref=part, send_sem=core_send.at[4],
-        recv_sem=core_recv.at[4], device_id=partner, device_id_type=MESH)
-    mark_copy = pltpu.make_async_remote_copy(
-        src_ref=mark, dst_ref=part_mark, send_sem=core_send.at[5],
-        recv_sem=core_recv.at[5], device_id=partner, device_id_type=MESH)
+        folded[number] = dot(parts_t[...], shift_cols[...])
+
+    backward(0)
     mark_copy.start()
-    roll(other)
-    part_copy.start()
+    backward(1, ((spread_pupil, 0),))
+    backward(2, ((spread_pupil, 1),))
+    backward(3, ((spread_pupil, 2),))
+    mark_copy.wait()
+    roll(grads[core], mark, 0)
+    advance(0, 0)
+    grad_copy(0).wait()
+    grad_copy(1).wait()
+    roll(peer_grad[...], part_mark, 1)
     spread_pupil(3)
-    roll(core)
-    part_copy.wait()
-    mark_copy.wait()
 
     iota_r = lax.broadcasted_iota(jnp.int32, (8, 128), 0).astype(F32)
     iota_c = lax.broadcasted_iota(jnp.int32, (8, 128), 1).astype(F32)
 
     def window(yx, carry):
-        bit_sets = [bits_of(yx // 4, yx % 4, zz) for zz in range(4)]
         for zz in range(2):
             for g in range(2):
                 base = 256 * zz + yx * 16 + g * 8
@@ -429,8 +467,8 @@
                     col_no = iota_c + float(block * 128)
                     col_a = col_no < mark[1]
                     col_b = col_no < part_mark[1]
-                    value_a = folded[core, rows, cols]
-                    value_b = part[rows, cols]
+                    value_a = folded[0, rows, cols]
+                    value_b = folded[1, rows, cols]
                     ra1 = jnp.where(row_a, value_a, 0.0)
                     ra0 = value_a - ra1
                     rb1 = jnp.where(row_b, value_b, 0.0)
@@ -439,22 +477,22 @@
                         va1 = jnp.where(col_a, va, 0.0)
                         vb1 = jnp.where(col_b, vb, 0.0)
                         tiles = ((va - va1) + (vb - vb1), va1 + vb1)
-                        bits = bit_sets[2 * upper + zz]
+                        at = {"y": yx // 4, "x": yx % 4, "z": 2 * upper + zz}
                         for later in range(2):
                             stream, unit = PLACE[CANVAS, g * 8 + later * 4 + block]
-                            own[stream][unit, slot_of(bits, stream)] = tiles[later]
+                            own[stream][unit, slot_of(at, stream)] = tiles[later]
         return carry
 
     lax.fori_loop(0, 16, window, 0)
     launch(CANVAS)
 
-    for phase, step in ((0, 0), (0, 1), (1, 0), (0, 2), (1, 1), (0, 3), (1, 2), (0, 4), (1, 3), (0, 5)):
+    for phase, step in BEFORE:
         advance(phase, step)
 
     for m in range(MODES):
         for g in range(4):
             stream, unit = PLACE[m, g]
-            pupil_src[m, g * 8:(g + 1) * 8, :] = own[stream][unit, ranges[stream][1]]
+            pupil_src[m, g * 8:(g + 1) * 8, :] = own[stream][unit, final_slot(stream)]
     block = pl.ds(pl.multiple_of((core * 4 + z) * 128, 128), 128)
     copies = []
     for number, (c, d) in enumerate(column):
@@ -467,13 +505,13 @@
         copies[-1].start()
     out_pup[:, :, block] = pupil_src[:, pl.ds(pl.multiple_of(core * 16, 16), 16), :]
 
-    for step in (4, 5):
-        advance(1, step)
+    for phase, step in AFTER:
+        advance(phase, step)
 
     for g in range(2):
         for b in range(8):
             stream, unit = PLACE[CANVAS, g * 8 + b]
-            canvas_src[g, :, b * 128:(b + 1) * 128] = own[stream][unit, ranges[stream][1]]
+            canvas_src[g, :, b * 128:(b + 1) * 128] = own[stream][unit, final_slot(stream)]
     half_cols = pl.ds(pl.multiple_of(core * SPEC, SPEC), SPEC)
     last = pltpu.make_async_remote_copy(
         src_ref=canvas_src.at[other], dst_ref=out_spec.at[0, :, half_cols],
@@ -497,7 +535,7 @@
             pltpu.VMEM((2, N + 24, N), F32),
             pltpu.SemaphoreType.DMA((2,)),
         ],
-        compiler_params=pltpu.CompilerParams(vmem_limit_bytes=16 * 2**20),
+        compiler_params=pltpu.CompilerParams(vmem_limit_bytes=60 * 2**20),
     )(offsets, spectrum)
     half, half_t, swap = (jnp.asarray(table) for table in tables())
     scratch = [
@@ -517,20 +555,21 @@
         pltpu.VMEM((MODES, N, N), F32),
         pltpu.VMEM((MODES, 32, 128), F32),
         pltpu.VMEM((2, 8, SPEC), F32),
+        pltpu.VMEM((MODES, N, 2 * N), BF16),
     ]
     scratch += [pltpu.VMEM((count, 64, 8, 128), F32) for count in COUNTS]
     scratch += [pltpu.VMEM((count, 63, 8, 128), F32) for count in COUNTS]
-    scratch += [pltpu.SemaphoreType.DMA((6,)), pltpu.SemaphoreType.DMA((6,))]
+    scratch += [pltpu.SemaphoreType.DMA((11,)), pltpu.SemaphoreType.DMA((11,))]
     scratch += [pltpu.SemaphoreType.DMA((len(PIECES), STREAMS)), pltpu.SemaphoreType.DMA((len(PIECES), STREAMS))]
-    scratch += [pltpu.SemaphoreType.DMA((len(PHASES), STREAMS, 6)), pltpu.SemaphoreType.DMA((len(PHASES), STREAMS, 6))]
-    scratch += [pltpu.SemaphoreType.DMA((8,)), pltpu.SemaphoreType.DMA((8,))]
+    scratch += [pltpu.SemaphoreType.DMA((len(PHASES), STREAMS, 7)), pltpu.SemaphoreType.DMA((len(PHASES), STREAMS, 7))]
+    scratch += [pltpu.SemaphoreType.DMA((8,)), pltpu.SemaphoreType.DMA((8,)), pltpu.SemaphoreType.DMA((MODES,))]
     return tuple(pl.pallas_call(
         kernel,
         out_shape=(
             jax.ShapeDtypeStruct((1, 8, 2 * SPEC), F32),
             jax.ShapeDtypeStruct((MODES, 16, 2 * N), F32),
         ),
-        in_specs=[vmem] * 7,
+        in_specs=[vmem] * 2 + [pl.BlockSpec(memory_space=pl.ANY)] + [vmem] * 4,
         out_specs=(vmem, vmem),
         scratch_shapes=scratch,
         compiler_params=pltpu.CompilerParams(

time: 86.8 us -> 78.9 us (0.909)
  local copies, waits for them, and re-layouts: 7.54 us -> 3.14 us
  Pallas kernels: 78.3 us -> 74.8 us
    pallas_call x1, Pallas kernels: 74.9 us -> 69.4 us  [local(): pl.pallas_call(kernel, out_shape=(jax.ShapeDtypeStruct((1, 8, 2 * SPEC),...]
    unnamed x10 -> x2, local copies, waits for them, and re-layouts: 7.54 us -> 3.14 us
    pallas_call x1, Pallas kernels: 3.45 us -> 5.45 us  [local(): pl.pallas_call(extract, out_shape=(jax.ShapeDtypeStruct((N, 2 * N), BF16)...]
where the time goes in v2:
time: 78.9 us; the launch traced here: 78.6 us
  Pallas kernels  74.8 us (95%)
  local copies, waits for them, and re-layouts  3.14 us (4%)
    pallas_call x1, Pallas kernels, local(): pl.pallas_call(kernel, out_shape=(jax.ShapeDtypeStruct((1, 8, 2 * SPEC),...  69.4 us
    pallas_call x1, Pallas kernels, local(): pl.pallas_call(extract, out_shape=(jax.ShapeDtypeStruct((N, 2 * N), BF16)...  5.45 us
    unnamed x2, local copies, waits for them, and re-layouts  3.14 us

profile of v2, /device:TPU:1, one launch (start us, length us, event | category | flops | bytes accessed | tf_op | source)
XLA Modules:
  0.0 78.6 jit_solution(11820131241605636323)
XLA Ops:
  0.6 5.5 %shard_map.86 = (bf16[512,1024]{1,0:T(8,128)(2,1)}, f32[2,8,128]{2,1,0:T(8,128)}) custom-call(s32[1,2]{1,0:T(1,128)} %offs.1, bf16[1024,2048]{1,0:T(8,128)(2,1)} %spectrum.1), custom_call_target="tpu_custom_call" | custom-call | tf_op jit(solution)/shard_map/pallas_call | solution.py:528
  6.1 69.4 %shard_map.87 = (f32[1,8,2048]{2,1,0:T(8,128)}, f32[4,16,1024]{2,1,0:T(8,128)}) custom-call(f32[2,8,128]{2,1,0:T(8,128)} %get-tuple-element.4.mark, bf16[512,1024]{1,0:T(8,128)(2,1)} %get-tuple-element.5.patch, bf16[4,512,1024]{2,1,0:T(8,128)(2,1)} %pupils.1, bf16[1,512,512]{2,1,0:T(8,128)(2,1)} %meas.1, bf16[512,512]{1,0:T(8,128)(2,1)} %constant.6.clone.tab, ...), custom_call_target="tpu_custom_call" | custom-call | tf_op jit(solution)/shard_map/pallas_call | solution.py:566
  75.5 1.5 %copy.11 = f32[1,8,2048]{2,1,0:T(8,128)} copy(f32[1,8,2048]{2,1,0:T(8,128)} %get-tuple-element.8) | data formatting | bytes 131072
  76.9 1.7 %copy.12 = f32[4,16,1024]{2,1,0:T(8,128)} copy(f32[4,16,1024]{2,1,0:T(8,128)} %get-tuple-element.9) | data formatting | bytes 524288

commit v3 on v2

--- a/solution.py
+++ b/solution.py
@@ -87,53 +87,29 @@
     return jnp.dot(a, b, preferred_element_type=F32)
 
 
-def extract(offs, spectrum, patch, mark, window, aligned, sem):
-    row, col = offs[0, 0], offs[0, 1]
-    row_from = pl.multiple_of(jnp.minimum(row // 16 * 16, N - 16), 16)
-    col_from = pl.multiple_of(jnp.minimum(col // 128 * 128, N - 128), 128)
-    copies = [
-        pltpu.make_async_copy(
-            spectrum.at[pl.ds(row_from, N + 16), pl.ds(part * SPEC + col_from, N + 128)],
-            window.at[part], sem.at[part])
-        for part in range(2)
-    ]
-    for copy in copies:
-        copy.start()
-    mark[0] = jnp.full((8, 128), row, jnp.int32).astype(F32)
-    mark[1] = jnp.full((8, 128), col, jnp.int32).astype(F32)
-    down = row - row_from
-    up = (24 - down % 8) % 24
-    turn = (N + 128 - (col - col_from)) % (N + 128)
-    for part in range(2):
-        copies[part].wait()
-
-        def turn_rows(i, carry):
-            rows = pl.ds(pl.multiple_of(i * 16, 16), 16)
-            aligned[part, rows, :] = pltpu.roll(window[part, rows, :].astype(F32), turn, 1)[:, :N]
-            return carry
-
-        lax.fori_loop(0, N // 16 + 1, turn_rows, 0, unroll=3)
-
-        def move_rows(i, carry):
-            rows = pl.ds(pl.multiple_of(i * 16, 16), 16)
-            source = pl.ds(pl.multiple_of((i * 2 + down // 8) * 8, 8), 24)
-            patch[rows, part * N:(part + 1) * N] = pltpu.roll(aligned[part, source, :], up, 0)[:16].astype(BF16)
-            return carry
-
-        lax.fori_loop(0, N // 16, move_rows, 0, unroll=4)
-
-
-def kernel(mark, patch, pupils, meas, tab, tabt, swap, out_spec, out_pup, *scratch):
-    (half_s, field, inten, measp, xs, grads, folded, shift_rows, shift_cols, parts, parts_t, peer_grad, part_mark,
-     peer, pupil_src, canvas_src, pup) = scratch[:17]
-    own = scratch[17:23]
-    landed = scratch[23:29]
-    (core_send, core_recv, send0, recv0, send, recv, gather_send, gather_recv, load) = scratch[29:]
+def kernel(offs, spectrum, pupils, measured, table, table_t, swap_in, out_spec, out_pup, *scratch):
+    (half_s, field, inten, measp, folds, grads, folded, shift_rows, shift_cols, parts, parts_t, peer_grad, part_mark,
+     peer, pupil_src, canvas_src, pup, mark, patch, whole, meas, tab, tabt, swap, pick_row, pick_col) = scratch[:26]
+    own = scratch[26:32]
+    landed = scratch[32:38]
+    (core_send, core_recv, send0, recv0, send, recv, gather_send, gather_recv, load) = scratch[38:]
 
     def pupil_load(m):
         return pltpu.make_async_copy(pupils.at[m], pup.at[m], load.at[m])
 
-    for m in range(MODES):
+    loads = [
+        pltpu.make_async_copy(source, target, load.at[MODES + number])
+        for number, (source, target) in enumerate((
+            (spectrum.at[:, :SPEC], whole.at[:, :SPEC]), (table, tab), (table_t, tabt), (measured, meas), (swap_in, swap),
+            (spectrum.at[:, SPEC:], whole.at[:, SPEC:])))
+    ]
+    loads[0].start()
+    loads[5].start()
+    loads[1].start()
+    pupil_load(0).start()
+    for copy in loads[2:5]:
+        copy.start()
+    for m in range(1, MODES):
         pupil_load(m).start()
 
 
@@ -168,10 +144,24 @@
     for target in greeted:
         pl.semaphore_signal(barrier, inc=1, device_id=target, device_id_type=MESH)
 
-    measp[:, :H] = meas[0, :, :H]
-    measp[:, H:] = dot(meas[0, :, H:], swap[...]).astype(BF16)
-    measp[H:, :] = dot(swap[...], measp[H:, :]).astype(BF16)
+    mark[0] = jnp.broadcast_to(offs[:, 0:1], (8, 128)).astype(F32)
+    mark[1] = jnp.broadcast_to(offs[:, 1:2], (8, 128)).astype(F32)
+    rise = lax.broadcasted_iota(jnp.int32, (N, 128), 1) - lax.broadcasted_iota(jnp.int32, (N, 128), 0)
+    fall = lax.broadcasted_iota(jnp.int32, (SPEC, 128), 0) - lax.broadcasted_iota(jnp.int32, (SPEC, 128), 1)
+    for b in range(8):
+        pick_row[:, b * 128:(b + 1) * 128] = (
+            rise.astype(F32) == mark[0, :1, :] - float(b * 128)).astype(F32).astype(BF16)
+    for b in range(4):
+        pick_col[:, b * 128:(b + 1) * 128] = (
+            fall.astype(F32) == mark[1, :1, :] + float(b * 128)).astype(F32).astype(BF16)
+    for number in range(2):
+        loads[5 * number].wait()
+        window = dot(pick_row[...], whole[:, number * SPEC:(number + 1) * SPEC]).astype(BF16)
+        patch[:, number * N:(number + 1) * N] = dot(window, pick_col[...]).astype(BF16)
+
     inten[...] = jnp.zeros_like(inten)
+    for copy in loads[1:3]:
+        copy.wait()
 
     lane0 = lax.broadcasted_iota(jnp.int32, (1, 128), 1) == 0
     row0 = lax.broadcasted_iota(jnp.int32, (16, 1), 0) == 0
@@ -222,6 +212,12 @@
 
     lax.fori_loop(0, MODES, forward, 0)
 
+    for copy in loads[3:5]:
+        copy.wait()
+    measp[:, :H] = meas[0, :, :H]
+    measp[:, H:] = dot(meas[0, :, H:], swap[...]).astype(BF16)
+    measp[H:, :] = dot(swap[...], measp[H:, :]).astype(BF16)
+
     def weigh(i, carry):
         rows = pl.ds(pl.multiple_of(i * 64, 64), 64)
         level = measp[rows, :].astype(F32)
@@ -231,9 +227,10 @@
     lax.fori_loop(0, N // 64, weigh, 0)
 
     def weigh_fold(m):
-        def fold(i, carry):
-            top = pl.ds(pl.multiple_of(i * 32, 32), 32)
-            bottom = pl.ds(pl.multiple_of(H + i * 32, 32), 32)
+        xs = folds.at[m % 2]
+        for i in range(H // 32):
+            top = slice(i * 32, i * 32 + 32)
+            bottom = slice(H + i * 32, H + i * 32 + 32)
             wt, wb = inten[top, :], inten[bottom, :]
             rt, rb = wt * field[0, m, top, :], wb * field[0, m, bottom, :]
             it, ib = wt * field[1, m, top, :], wb * field[1, m, bottom, :]
@@ -241,9 +238,6 @@
             xs[0, bottom, :] = (it - ib).astype(BF16)
             xs[1, top, :] = (it + ib).astype(BF16)
             xs[1, bottom, :] = (rb - rt).astype(BF16)
-            return carry
-
-        lax.fori_loop(0, H // 32, fold, 0)
         wt, wb = inten[:16, :], inten[H:H + 16, :]
         rt, rb = wt * field[0, m, :16, :], wb * field[0, m, H:H + 16, :]
         it, ib = wt * field[1, m, :16, :], wb * field[1, m, H:H + 16, :]
@@ -253,6 +247,7 @@
         xs[1, H:H + 16, :] = jnp.where(row0, ib, rb - rt).astype(BF16)
 
     def transform(m, i):
+        xs = folds.at[m % 2]
         rows = slice(i * H, (i + 1) * H)
         fr = dot(tabt[rows, :], xs[0])
         fi = dot(tabt[rows, :], xs[1])
@@ -525,25 +520,13 @@
 
 def local(spectrum, pupils, offsets, measured):
     vmem = pl.BlockSpec(memory_space=pltpu.VMEM)
-    patch, mark = pl.pallas_call(
-        extract,
-        out_shape=(jax.ShapeDtypeStruct((N, 2 * N), BF16), jax.ShapeDtypeStruct((2, 8, 128), F32)),
-        in_specs=[pl.BlockSpec(memory_space=pltpu.SMEM), pl.BlockSpec(memory_space=pl.ANY)],
-        out_specs=(vmem, vmem),
-        scratch_shapes=[
-            pltpu.VMEM((2, N + 16, N + 128), BF16),
-            pltpu.VMEM((2, N + 24, N), F32),
-            pltpu.SemaphoreType.DMA((2,)),
-        ],
-        compiler_params=pltpu.CompilerParams(vmem_limit_bytes=60 * 2**20),
-    )(offsets, spectrum)
     half, half_t, swap = (jnp.asarray(table) for table in tables())
     scratch = [
         pltpu.VMEM((2, N, N), BF16),
         pltpu.VMEM((2, MODES, N, N), F32),
         pltpu.VMEM((N, N), F32),
         pltpu.VMEM((N, N), BF16),
-        pltpu.VMEM((2, N, N), BF16),
+        pltpu.VMEM((2, 2, N, N), BF16),
         pltpu.VMEM((2, N, N), F32),
         pltpu.VMEM((2, N, N), F32),
         pltpu.VMEM((N, 2 * N), BF16),
@@ -556,25 +539,34 @@
         pltpu.VMEM((MODES, 32, 128), F32),
         pltpu.VMEM((2, 8, SPEC), F32),
         pltpu.VMEM((MODES, N, 2 * N), BF16),
+        pltpu.VMEM((2, 8, 128), F32),
+        pltpu.VMEM((N, 2 * N), BF16),
+        pltpu.VMEM((SPEC, 2 * SPEC), BF16),
+        pltpu.VMEM((1, N, N), BF16),
+        pltpu.VMEM((N, N), BF16),
+        pltpu.VMEM((N, N), BF16),
+        pltpu.VMEM((H, H), BF16),
+        pltpu.VMEM((N, SPEC), BF16),
+        pltpu.VMEM((SPEC, N), BF16),
     ]
     scratch += [pltpu.VMEM((count, 64, 8, 128), F32) for count in COUNTS]
     scratch += [pltpu.VMEM((count, 63, 8, 128), F32) for count in COUNTS]
     scratch += [pltpu.SemaphoreType.DMA((11,)), pltpu.SemaphoreType.DMA((11,))]
     scratch += [pltpu.SemaphoreType.DMA((len(PIECES), STREAMS)), pltpu.SemaphoreType.DMA((len(PIECES), STREAMS))]
     scratch += [pltpu.SemaphoreType.DMA((len(PHASES), STREAMS, 7)), pltpu.SemaphoreType.DMA((len(PHASES), STREAMS, 7))]
-    scratch += [pltpu.SemaphoreType.DMA((8,)), pltpu.SemaphoreType.DMA((8,)), pltpu.SemaphoreType.DMA((MODES,))]
+    scratch += [pltpu.SemaphoreType.DMA((8,)), pltpu.SemaphoreType.DMA((8,)), pltpu.SemaphoreType.DMA((MODES + 6,))]
     return tuple(pl.pallas_call(
         kernel,
         out_shape=(
             jax.ShapeDtypeStruct((1, 8, 2 * SPEC), F32),
             jax.ShapeDtypeStruct((MODES, 16, 2 * N), F32),
         ),
-        in_specs=[vmem] * 2 + [pl.BlockSpec(memory_space=pl.ANY)] + [vmem] * 4,
+        in_specs=[vmem] + [pl.BlockSpec(memory_space=pl.ANY)] * 6,
         out_specs=(vmem, vmem),
         scratch_shapes=scratch,
         compiler_params=pltpu.CompilerParams(
             collective_id=0, has_side_effects=True, vmem_limit_bytes=60 * 2**20),
-    )(mark, patch, pupils, measured, half, half_t, swap))
+    )(offsets, spectrum, pupils, measured, half, half_t, swap))
 
 
 def solution(mesh):

time: 78.9 us -> 76.9 us (0.975)
  Pallas kernels: 74.8 us -> 72.9 us
    pallas_call x1 -> x0, Pallas kernels: 5.45 us -> none  [local(): pl.pallas_call(extract, out_shape=(jax.ShapeDtypeStruct((N, 2 * N), BF16)...]
    pallas_call x1, Pallas kernels: 69.4 us -> 72.9 us  [local(): pl.pallas_call(kernel, out_shape=(jax.ShapeDtypeStruct((1, 8, 2 * SPEC),...]
where the time goes in v3:
time: 76.9 us; the launch traced here: 76.7 us
  Pallas kernels  72.9 us (95%)
  local copies, waits for them, and re-layouts  3.14 us (4%)
    pallas_call x1, Pallas kernels, local(): pl.pallas_call(kernel, out_shape=(jax.ShapeDtypeStruct((1, 8, 2 * SPEC),...  72.9 us
    unnamed x2, local copies, waits for them, and re-layouts  3.14 us

profile of v3, /device:TPU:1, one launch (start us, length us, event | category | flops | bytes accessed | tf_op | source)
XLA Modules:
  0.0 76.7 jit_solution(16012560513540676088)
XLA Ops:
  0.6 72.9 %shard_map.86 = (f32[1,8,2048]{2,1,0:T(8,128)}, f32[4,16,1024]{2,1,0:T(8,128)}) custom-call(s32[1,2]{1,0:T(1,128)} %offs.1, bf16[1024,2048]{1,0:T(8,128)(2,1)} %spectrum.1, bf16[4,512,1024]{2,1,0:T(8,128)(2,1)} %pupils.1, bf16[1,512,512]{2,1,0:T(8,128)(2,1)} %measured.1, bf16[512,512]{1,0:T(8,128)(2,1)} %constant.6.clone.table, ...), custom_call_target="tpu_custom_call" | custom-call | tf_op jit(solution)/shard_map/pallas_call | solution.py:558
  73.6 1.5 %copy.11 = f32[1,8,2048]{2,1,0:T(8,128)} copy(f32[1,8,2048]{2,1,0:T(8,128)} %get-tuple-element.4) | data formatting | bytes 131072
  75.0 1.7 %copy.12 = f32[4,16,1024]{2,1,0:T(8,128)} copy(f32[4,16,1024]{2,1,0:T(8,128)} %get-tuple-element.5) | data formatting | bytes 524288

commit v4 on v3

--- a/solution.py
+++ b/solution.py
@@ -22,11 +22,11 @@
 
 STREAMS = 6
 PIECES = (
-    (0, 1, 2, 3),
-    (4, 5, 0, 1),
-    (2, 3, 4, 5),
-    (0, 1, 2, 3),
-    (0, 1, 2, 3, 4, 4, 5, 5, 0, 1, 2, 2, 3, 3, 4, 5),
+    (3, 4, 4, 5),
+    (0, 1, 2, 5),
+    (0, 2, 3, 5),
+    (3, 4, 4, 5),
+    (0, 0, 0, 1, 1, 1, 2, 2, 2, 3, 3, 4, 4, 5, 5, 5),
 )
 CANVAS = 4
 PHASES = ((0, 1), (2, 3), (4,))
@@ -518,6 +518,11 @@
     last.wait()
 
 
+def hand_over(spec_in, pup_in, spec_out, pup_out):
+    spec_out[...] = spec_in[...]
+    pup_out[...] = pup_in[...]
+
+
 def local(spectrum, pupils, offsets, measured):
     vmem = pl.BlockSpec(memory_space=pltpu.VMEM)
     half, half_t, swap = (jnp.asarray(table) for table in tables())
@@ -555,7 +560,7 @@
     scratch += [pltpu.SemaphoreType.DMA((len(PIECES), STREAMS)), pltpu.SemaphoreType.DMA((len(PIECES), STREAMS))]
     scratch += [pltpu.SemaphoreType.DMA((len(PHASES), STREAMS, 7)), pltpu.SemaphoreType.DMA((len(PHASES), STREAMS, 7))]
     scratch += [pltpu.SemaphoreType.DMA((8,)), pltpu.SemaphoreType.DMA((8,)), pltpu.SemaphoreType.DMA((MODES + 6,))]
-    return tuple(pl.pallas_call(
+    outs = tuple(pl.pallas_call(
         kernel,
         out_shape=(
             jax.ShapeDtypeStruct((1, 8, 2 * SPEC), F32),
@@ -567,6 +572,12 @@
         compiler_params=pltpu.CompilerParams(
             collective_id=0, has_side_effects=True, vmem_limit_bytes=60 * 2**20),
     )(offsets, spectrum, pupils, measured, half, half_t, swap))
+    return tuple(pl.pallas_call(
+        hand_over,
+        out_shape=tuple(jax.ShapeDtypeStruct(out.shape, F32) for out in outs),
+        in_specs=[vmem] * 2,
+        out_specs=(vmem, vmem),
+    )(*outs))
 
 
 def solution(mesh):

time: 76.9 us -> 73.7 us (0.958)
  local copies, waits for them, and re-layouts: 3.14 us -> 0 us
    unnamed x2 -> x0, local copies, waits for them, and re-layouts: 3.14 us -> none
    pallas_call x0 -> x1, Pallas kernels: none -> 1.72 us  [local(): pl.pallas_call(hand_over, out_shape=tuple((jax.ShapeDtypeStruct(out.shape...]
    pallas_call x1, Pallas kernels: 72.9 us -> 71.2 us  [local(): pl.pallas_call(kernel, out_shape=(jax.ShapeDtypeStruct((1, 8, 2 * SPEC),...]
where the time goes in v4:
time: 73.7 us; the launch traced here: 73.6 us
  Pallas kernels  72.9 us (99%)
    pallas_call x1, Pallas kernels, local(): pl.pallas_call(kernel, out_shape=(jax.ShapeDtypeStruct((1, 8, 2 * SPEC),...  71.2 us
    pallas_call x1, Pallas kernels, local(): pl.pallas_call(hand_over, out_shape=tuple((jax.ShapeDtypeStruct(out.shape...  1.72 us

profile of v4, /device:TPU:1, one launch (start us, length us, event | category | flops | bytes accessed | tf_op | source)
XLA Modules:
  0.0 73.6 jit_solution(16977945136109378966)
XLA Ops:
  0.6 71.2 %shard_map.86 = (f32[1,8,2048]{2,1,0:T(8,128)}, f32[4,16,1024]{2,1,0:T(8,128)}) custom-call(s32[1,2]{1,0:T(1,128)} %offs.1, bf16[1024,2048]{1,0:T(8,128)(2,1)} %spectrum.1, bf16[4,512,1024]{2,1,0:T(8,128)(2,1)} %pupils.1, bf16[1,512,512]{2,1,0:T(8,128)(2,1)} %measured.1, bf16[512,512]{1,0:T(8,128)(2,1)} %constant.6.clone.table, ...), custom_call_target="tpu_custom_call" | custom-call | tf_op jit(solution)/shard_map/pallas_call | solution.py:563
  71.9 1.7 %shard_map.87 = (f32[1,8,2048]{2,1,0:T(8,128)}, f32[4,16,1024]{2,1,0:T(8,128)}) custom-call(f32[1,8,2048]{2,1,0:T(8,128)} %get-tuple-element.4.spec_in, f32[4,16,1024]{2,1,0:T(8,128)} %get-tuple-element.5.pup_in), custom_call_target="tpu_custom_call" | custom-call | tf_op jit(solution)/shard_map/pallas_call | solution.py:575

commit v5 on v4

--- a/solution.py
+++ b/solution.py
@@ -363,21 +363,27 @@
                 for copy in hops(phase, stream, step + 1):
                     copy.start()
 
+    def y_slots(yy):
+        return [slot_of({"y": yy, "x": 0, "z": 0}, stream) for stream in range(STREAMS)]
+
     def spread_pupil(m):
         core_copy(m, 0).wait()
         core_copy(m, 1).wait()
 
-        def body(yx, carry):
-            for zz in range(4):
-                at = {"y": yx // 4, "x": yx % 4, "z": zz}
-                cols = slice(zz * 128, (zz + 1) * 128)
-                for g in range(4):
-                    stream, unit = PLACE[m, g]
-                    rows = pl.ds(pl.multiple_of(yx * 32 + g * 8, 8), 8)
-                    own[stream][unit, slot_of(at, stream)] = field[core, m, rows, cols] + peer[m, rows, cols]
+        def body(yy, carry):
+            begin = y_slots(yy)
+            for xx in range(4):
+                for zz in range(4):
+                    at = {"y": 0, "x": xx, "z": zz}
+                    cols = slice(zz * 128, (zz + 1) * 128)
+                    for g in range(4):
+                        stream, unit = PLACE[m, g]
+                        rows = pl.ds(pl.multiple_of(yy * 128 + (xx * 32 + g * 8), 8), 8)
+                        slot = begin[stream] + slot_of(at, stream)
+                        own[stream][unit, slot] = field[core, m, rows, cols] + peer[m, rows, cols]
             return carry
 
-        lax.fori_loop(0, 16, body, 0)
+        lax.fori_loop(0, 4, body, 0)
         launch(m)
 
     def grad_copy(i):
@@ -449,36 +455,38 @@
     iota_r = lax.broadcasted_iota(jnp.int32, (8, 128), 0).astype(F32)
     iota_c = lax.broadcasted_iota(jnp.int32, (8, 128), 1).astype(F32)
 
-    def window(yx, carry):
-        for zz in range(2):
-            for g in range(2):
-                base = 256 * zz + yx * 16 + g * 8
-                rows = pl.ds(pl.multiple_of(base, 8), 8)
-                row_no = iota_r + base.astype(F32)
-                row_a = row_no < mark[0]
-                row_b = row_no < part_mark[0]
-                for block in range(4):
-                    cols = slice(block * 128, (block + 1) * 128)
-                    col_no = iota_c + float(block * 128)
-                    col_a = col_no < mark[1]
-                    col_b = col_no < part_mark[1]
-                    value_a = folded[0, rows, cols]
-                    value_b = folded[1, rows, cols]
-                    ra1 = jnp.where(row_a, value_a, 0.0)
-                    ra0 = value_a - ra1
-                    rb1 = jnp.where(row_b, value_b, 0.0)
-                    rb0 = value_b - rb1
-                    for upper, (va, vb) in enumerate(((ra0, rb0), (ra1, rb1))):
-                        va1 = jnp.where(col_a, va, 0.0)
-                        vb1 = jnp.where(col_b, vb, 0.0)
-                        tiles = ((va - va1) + (vb - vb1), va1 + vb1)
-                        at = {"y": yx // 4, "x": yx % 4, "z": 2 * upper + zz}
-                        for later in range(2):
-                            stream, unit = PLACE[CANVAS, g * 8 + later * 4 + block]
-                            own[stream][unit, slot_of(at, stream)] = tiles[later]
+    def window(yy, carry):
+        begin = y_slots(yy)
+        for xx in range(4):
+            for zz in range(2):
+                for g in range(2):
+                    base = yy * 64 + (256 * zz + xx * 16 + g * 8)
+                    rows = pl.ds(pl.multiple_of(base, 8), 8)
+                    row_no = iota_r + base.astype(F32)
+                    row_a = row_no < mark[0]
+                    row_b = row_no < part_mark[0]
+                    for block in range(4):
+                        cols = slice(block * 128, (block + 1) * 128)
+                        col_no = iota_c + float(block * 128)
+                        col_a = col_no < mark[1]
+                        col_b = col_no < part_mark[1]
+                        value_a = folded[0, rows, cols]
+                        value_b = folded[1, rows, cols]
+                        ra1 = jnp.where(row_a, value_a, 0.0)
+                        ra0 = value_a - ra1
+                        rb1 = jnp.where(row_b, value_b, 0.0)
+                        rb0 = value_b - rb1
+                        for upper, (va, vb) in enumerate(((ra0, rb0), (ra1, rb1))):
+                            va1 = jnp.where(col_a, va, 0.0)
+                            vb1 = jnp.where(col_b, vb, 0.0)
+                            tiles = ((va - va1) + (vb - vb1), va1 + vb1)
+                            at = {"y": 0, "x": xx, "z": 2 * upper + zz}
+                            for later in range(2):
+                                stream, unit = PLACE[CANVAS, g * 8 + later * 4 + block]
+                                own[stream][unit, begin[stream] + slot_of(at, stream)] = tiles[later]
         return carry
 
-    lax.fori_loop(0, 16, window, 0)
+    lax.fori_loop(0, 4, window, 0)
     launch(CANVAS)
 
     for phase, step in BEFORE:

time: 73.7 us -> 71.8 us (0.974)
  Pallas kernels: 72.9 us -> 71 us
    pallas_call x1, Pallas kernels: 71.2 us -> 69.3 us  [local(): pl.pallas_call(kernel, out_shape=(jax.ShapeDtypeStruct((1, 8, 2 * SPEC),...]
where the time goes in v5:
time: 71.8 us; the launch traced here: 71.6 us
  Pallas kernels  71 us (99%)
    pallas_call x1, Pallas kernels, local(): pl.pallas_call(kernel, out_shape=(jax.ShapeDtypeStruct((1, 8, 2 * SPEC),...  69.3 us
    pallas_call x1, Pallas kernels, local(): pl.pallas_call(hand_over, out_shape=tuple((jax.ShapeDtypeStruct(out.shape...  1.72 us

profile of v5, /device:TPU:1, one launch (start us, length us, event | category | flops | bytes accessed | tf_op | source)
XLA Modules:
  0.0 71.6 jit_solution(12468005943785293833)
XLA Ops:
  0.6 69.3 %shard_map.86 = (f32[1,8,2048]{2,1,0:T(8,128)}, f32[4,16,1024]{2,1,0:T(8,128)}) custom-call(s32[1,2]{1,0:T(1,128)} %offs.1, bf16[1024,2048]{1,0:T(8,128)(2,1)} %spectrum.1, bf16[4,512,1024]{2,1,0:T(8,128)(2,1)} %pupils.1, bf16[1,512,512]{2,1,0:T(8,128)(2,1)} %measured.1, bf16[512,512]{1,0:T(8,128)(2,1)} %constant.6.clone.table, ...), custom_call_target="tpu_custom_call" | custom-call | tf_op jit(solution)/shard_map/pallas_call | solution.py:571
  69.9 1.7 %shard_map.87 = (f32[1,8,2048]{2,1,0:T(8,128)}, f32[4,16,1024]{2,1,0:T(8,128)}) custom-call(f32[1,8,2048]{2,1,0:T(8,128)} %get-tuple-element.4.spec_in, f32[4,16,1024]{2,1,0:T(8,128)} %get-tuple-element.5.pup_in), custom_call_target="tpu_custom_call" | custom-call | tf_op jit(solution)/shard_map/pallas_call | solution.py:583

commit v6 on v5

--- a/solution.py
+++ b/solution.py
@@ -30,7 +30,7 @@
 )
 CANVAS = 4
 PHASES = ((0, 1), (2, 3), (4,))
-BEFORE = ((0, 1), (1, 0), (2, 0), (0, 2), (1, 1), (2, 1), (0, 3), (1, 2), (2, 2), (1, 3))
+BEFORE = ((1, 0), (0, 1), (2, 0), (0, 2), (1, 1), (2, 1), (0, 3), (1, 2), (2, 2), (1, 3))
 AFTER = ((2, 3),)
 
 
@@ -378,12 +378,13 @@
                     cols = slice(zz * 128, (zz + 1) * 128)
                     for g in range(4):
                         stream, unit = PLACE[m, g]
-                        rows = pl.ds(pl.multiple_of(yy * 128 + (xx * 32 + g * 8), 8), 8)
+                        rows = slice(yy * 128 + xx * 32 + g * 8, yy * 128 + xx * 32 + g * 8 + 8)
                         slot = begin[stream] + slot_of(at, stream)
                         own[stream][unit, slot] = field[core, m, rows, cols] + peer[m, rows, cols]
             return carry
 
-        lax.fori_loop(0, 4, body, 0)
+        for yy in range(4):
+            body(yy, 0)
         launch(m)
 
     def grad_copy(i):
@@ -461,8 +462,8 @@
             for zz in range(2):
                 for g in range(2):
                     base = yy * 64 + (256 * zz + xx * 16 + g * 8)
-                    rows = pl.ds(pl.multiple_of(base, 8), 8)
-                    row_no = iota_r + base.astype(F32)
+                    rows = slice(base, base + 8)
+                    row_no = iota_r + float(base)
                     row_a = row_no < mark[0]
                     row_b = row_no < part_mark[0]
                     for block in range(4):
@@ -486,7 +487,8 @@
                                 own[stream][unit, begin[stream] + slot_of(at, stream)] = tiles[later]
         return carry
 
-    lax.fori_loop(0, 4, window, 0)
+    for yy in range(4):
+        window(yy, 0)
     launch(CANVAS)
 
     for phase, step in BEFORE:

time: 71.8 us -> 71.1 us (level)
  no operation moved by 1% of the time
where the time goes in v6:
time: 71.1 us; the launch traced here: 70.9 us
  Pallas kernels  70.3 us (99%)
    pallas_call x1, Pallas kernels, local(): pl.pallas_call(kernel, out_shape=(jax.ShapeDtypeStruct((1, 8, 2 * SPEC),...  68.6 us
    pallas_call x1, Pallas kernels, local(): pl.pallas_call(hand_over, out_shape=tuple((jax.ShapeDtypeStruct(out.shape...  1.72 us

profile of v6, /device:TPU:1, one launch (start us, length us, event | category | flops | bytes accessed | tf_op | source)
XLA Modules:
  0.0 70.9 jit_solution(12508738216157840342)
XLA Ops:
  0.6 68.6 %shard_map.86 = (f32[1,8,2048]{2,1,0:T(8,128)}, f32[4,16,1024]{2,1,0:T(8,128)}) custom-call(s32[1,2]{1,0:T(1,128)} %offs.1, bf16[1024,2048]{1,0:T(8,128)(2,1)} %spectrum.1, bf16[4,512,1024]{2,1,0:T(8,128)(2,1)} %pupils.1, bf16[1,512,512]{2,1,0:T(8,128)(2,1)} %measured.1, bf16[512,512]{1,0:T(8,128)(2,1)} %constant.6.clone.table, ...), custom_call_target="tpu_custom_call" | custom-call | tf_op jit(solution)/shard_map/pallas_call | solution.py:573
  69.2 1.7 %shard_map.87 = (f32[1,8,2048]{2,1,0:T(8,128)}, f32[4,16,1024]{2,1,0:T(8,128)}) custom-call(f32[1,8,2048]{2,1,0:T(8,128)} %get-tuple-element.4.spec_in, f32[4,16,1024]{2,1,0:T(8,128)} %get-tuple-element.5.pup_in), custom_call_target="tpu_custom_call" | custom-call | tf_op jit(solution)/shard_map/pallas_call | solution.py:585

commit v7 on v6

--- a/solution.py
+++ b/solution.py
@@ -210,7 +210,7 @@
                 inten[rows, right] += rr * rr + ir * ir
         return carry
 
-    lax.fori_loop(0, MODES, forward, 0)
+    lax.fori_loop(0, MODES, forward, 0, unroll=2)
 
     for copy in loads[3:5]:
         copy.wait()
@@ -224,7 +224,7 @@
         inten[rows, :] = 1.0 - level * lax.rsqrt(level * jnp.maximum(inten[rows, :], 0.1))
         return carry
 
-    lax.fori_loop(0, N // 64, weigh, 0)
+    lax.fori_loop(0, N // 64, weigh, 0, unroll=8)
 
     def weigh_fold(m):
         xs = folds.at[m % 2]

time: 71.1 us -> 71.1 us (level)
  no operation moved by 1% of the time
where the time goes in v7:
time: 71.1 us; the launch traced here: 70.9 us
  Pallas kernels  70.3 us (99%)
    pallas_call x1, Pallas kernels, local(): pl.pallas_call(kernel, out_shape=(jax.ShapeDtypeStruct((1, 8, 2 * SPEC),...  68.6 us
    pallas_call x1, Pallas kernels, local(): pl.pallas_call(hand_over, out_shape=tuple((jax.ShapeDtypeStruct(out.shape...  1.72 us

profile of v7, /device:TPU:1, one launch (start us, length us, event | category | flops | bytes accessed | tf_op | source)
XLA Modules:
  0.0 70.9 jit_solution(6607752852146947938)
XLA Ops:
  0.6 68.6 %shard_map.86 = (f32[1,8,2048]{2,1,0:T(8,128)}, f32[4,16,1024]{2,1,0:T(8,128)}) custom-call(s32[1,2]{1,0:T(1,128)} %offs.1, bf16[1024,2048]{1,0:T(8,128)(2,1)} %spectrum.1, bf16[4,512,1024]{2,1,0:T(8,128)(2,1)} %pupils.1, bf16[1,512,512]{2,1,0:T(8,128)(2,1)} %measured.1, bf16[512,512]{1,0:T(8,128)(2,1)} %constant.6.clone.table, ...), custom_call_target="tpu_custom_call" | custom-call | tf_op jit(solution)/shard_map/pallas_call | solution.py:573
  69.2 1.7 %shard_map.87 = (f32[1,8,2048]{2,1,0:T(8,128)}, f32[4,16,1024]{2,1,0:T(8,128)}) custom-call(f32[1,8,2048]{2,1,0:T(8,128)} %get-tuple-element.4.spec_in, f32[4,16,1024]{2,1,0:T(8,128)} %get-tuple-element.5.pup_in), custom_call_target="tpu_custom_call" | custom-call | tf_op jit(solution)/shard_map/pallas_call | solution.py:585
